TPU v7x, 32 devices: a whole 2x2x4 slice. The times are simulated.
32 devices in a mesh: dp: 2 (over core), seq: 4 (over y, x), expert: 4 (over z).
Axes of the slice: x: 2, y: 2, z: 4, core: 2. Of those that a mesh axis runs over, the one named last changes fastest.
Arguments:
- query_input: bfloat16 [8, 512, 1024], P(('dp', 'expert'), 'seq'), may hold values from -6 to 6
- key_input: bfloat16 [8, 512, 1024], P(('dp', 'expert'), 'seq'), may hold values from -6 to 6
- value_input: bfloat16 [8, 512, 1024], P(('dp', 'expert'), 'seq'), may hold values from -6 to 6
- routes: int32 [8, 512, 2], P(('dp', 'expert'), 'seq'), may hold values from 0 to 3, all different within a row; in each aligned block of 128 rows (0 to 127, 128 to 255, ..., all dimensions but the last counted through in order) at most 96 rows name the same one
- gate_values: float32 [8, 512, 2], P(('dp', 'expert'), 'seq'), may hold values from 0.2 to 1
- up_weight: bfloat16 [4, 1024, 2048], P('expert'), may hold values from -0.1875 to 0.1875
- down_weight: bfloat16 [4, 2048, 1024], P('expert'), may hold values from -0.125 to 0.125
- cotangent: bfloat16 [8, 512, 1024], P(('dp', 'expert'), 'seq'), may hold values from -6 to 6
Outputs:
- layer_output: bfloat16 [8, 512, 1024], P(('dp', 'expert'), 'seq')
- grad_queries: bfloat16 [8, 512, 1024], P(('dp', 'expert'), 'seq')
- grad_keys: bfloat16 [8, 512, 1024], P(('dp', 'expert'), 'seq')
- grad_values: bfloat16 [8, 512, 1024], P(('dp', 'expert'), 'seq')
- grad_up: float32 [4, 1024, 2048], P('expert', ('dp', 'seq'))
- grad_down: float32 [4, 2048, 1024], P('expert', None, ('dp', 'seq'))
Inputs may be any that keep to these rules, and one draw needn't show every extreme that they name: `routes`: each token names 2 different experts. The 128 tokens of one device (aligned blocks of rows) name any one expert at most 96 times, and in every draw some device's tokens name some expert exactly 96 times.
All inputs are finite; a program needn't handle non-finite values.
Results may differ from a plain program's by a relative error of at most 0.017.
Values may be sent and summed in bfloat16 or wider, within the bound.
A program may use at most 128 MiB of HBM per device.

v0:
```python
import math

import jax
import jax.numpy as jnp
from jax import lax
from jax.sharding import PartitionSpec as P

DH = 128
TOP = 2


EPSILON = 1e-06
GELU_COEF = math.sqrt(2.0 / math.pi)


def gelu_pair(inputs):
    cubic = inputs + 0.044715 * inputs * inputs * inputs
    hyper = jnp.tanh(GELU_COEF * cubic)
    result = 0.5 * inputs * (1.0 + hyper)
    slope_value = 0.5 * (1.0 + hyper) + 0.5 * inputs * (1.0 - hyper * hyper) * GELU_COEF * (
        1.0 + 3.0 * 0.044715 * inputs * inputs
    )
    return (result, slope_value)


def prob_table(query_piece, key_rows):
    scaling = 1.0 / math.sqrt(query_piece.shape[2])
    scores = (
        jnp.einsum("qhd,khd->hqk", query_piece, key_rows, preferred_element_type=jnp.float32)
        * scaling
    )
    highest = jnp.max(scores, axis=-1, keepdims=True)
    exponent = jnp.exp(scores - highest)
    return exponent / jnp.sum(exponent, axis=-1, keepdims=True)


def query_blocks(tensor):
    row_count = tensor.shape[0]
    block_rows = min(512, row_count)
    return tensor.reshape((row_count // block_rows, block_rows) + tensor.shape[1:])


def attention_forward(query_rows, key_rows, value_rows):

    def one_block(query_piece):
        prob_rows = prob_table(query_piece, key_rows)
        prob_bf = prob_rows.astype(jnp.bfloat16)
        return jnp.einsum(
            "hqk,khd->qhd", prob_bf, value_rows, preferred_element_type=jnp.float32
        ).astype(jnp.bfloat16)

    return lax.map(one_block, query_blocks(query_rows)).reshape(query_rows.shape)


def attention_backward(query_rows, key_rows, value_rows, upstream):
    scaling = 1.0 / math.sqrt(query_rows.shape[2])

    def one_block(running, pieces):
        query_piece, grad_piece = pieces
        prob_rows = prob_table(query_piece, key_rows)
        prob_bf = prob_rows.astype(jnp.bfloat16)
        grad_probs = jnp.einsum(
            "qhd,khd->hqk", grad_piece, value_rows, preferred_element_type=jnp.float32
        )
        row_delta = jnp.sum(prob_rows * grad_probs, axis=-1, keepdims=True)
        grad_scores = (prob_rows * (grad_probs - row_delta) * scaling).astype(jnp.bfloat16)
        grad_query = jnp.einsum(
            "hqk,khd->qhd", grad_scores, key_rows, preferred_element_type=jnp.float32
        ).astype(jnp.bfloat16)
        grad_key = running[0] + jnp.einsum(
            "hqk,qhd->khd", grad_scores, query_piece, preferred_element_type=jnp.float32
        )
        grad_value = running[1] + jnp.einsum(
            "hqk,qhd->khd", prob_bf, grad_piece, preferred_element_type=jnp.float32
        )
        return ((grad_key, grad_value), grad_query)

    zero_grads = jnp.zeros(key_rows.shape, jnp.float32)
    (grad_key, grad_value), grad_query = lax.scan(
        one_block, (zero_grads, zero_grads), (query_blocks(query_rows), query_blocks(upstream))
    )
    return (grad_query.reshape(query_rows.shape), grad_key, grad_value)


def shards(
    query_input, key_input, value_input, routes, gate_values, up_weight, down_weight, cotangent
):
    tok_rows = query_input.shape[1]
    model_width = query_input.shape[2]
    owners = lax.axis_size("expert")
    local_experts = up_weight.shape[0]
    experts_all = local_experts * owners
    capacity = tok_rows * TOP * 3 // (2 * experts_all)
    query_local = query_input[0]
    key_local = key_input[0]
    value_local = value_input[0]
    query_heads, key_heads, value_heads = (
        lax.all_to_all(query_local, "seq", split_axis=1, concat_axis=0, tiled=True),
        lax.all_to_all(key_local, "seq", split_axis=1, concat_axis=0, tiled=True),
        lax.all_to_all(value_local, "seq", split_axis=1, concat_axis=0, tiled=True),
    )
    head_shape = (query_heads.shape[0], query_heads.shape[1] // DH, DH)
    query_split = query_heads.reshape(head_shape)
    key_split = key_heads.reshape(head_shape)
    value_split = value_heads.reshape(head_shape)
    out_heads = attention_forward(query_split, key_split, value_split).reshape(query_heads.shape)
    attended = lax.all_to_all(out_heads, "seq", split_axis=0, concat_axis=1, tiled=True)
    chosen = routes[0].reshape(-1)
    expert_ids = jnp.arange(experts_all, dtype=jnp.int32)
    hit_table = (chosen[:, None] == expert_ids[None, :]).astype(jnp.int32)
    slot_rank = jnp.sum((jnp.cumsum(hit_table, axis=0) - hit_table) * hit_table, axis=1)
    slot_index = chosen * capacity + slot_rank
    slot_ids = jnp.arange(experts_all * capacity, dtype=jnp.int32)
    placer = (slot_index[:, None] == slot_ids[None, :]).astype(jnp.bfloat16)

    def send_rows(assigned):
        packed = lax.dot_general(
            placer, assigned, (((0,), (0,)), ((), ())), preferred_element_type=jnp.float32
        ).astype(jnp.bfloat16)
        arrived_rows = lax.all_to_all(
            packed.reshape(owners, local_experts * capacity, model_width),
            "expert",
            split_axis=0,
            concat_axis=0,
            tiled=True,
        )
        return arrived_rows.reshape(owners, local_experts, capacity, model_width)

    def return_rows(results):
        returned_rows = lax.all_to_all(
            results.reshape(owners, local_experts * capacity, model_width),
            "expert",
            split_axis=0,
            concat_axis=0,
            tiled=True,
        )
        flat_rows = returned_rows.reshape(experts_all * capacity, model_width)
        return jnp.dot(placer, flat_rows, preferred_element_type=jnp.float32).reshape(
            tok_rows, TOP, model_width
        )

    attended_f = attended.astype(jnp.float32)
    inverse_rms = lax.rsqrt(jnp.mean(attended_f * attended_f, axis=-1, keepdims=True) + EPSILON)
    unit_rows = attended_f * inverse_rms
    normed = unit_rows.astype(jnp.bfloat16)
    arrived = send_rows(jnp.repeat(normed, TOP, axis=0))
    pre_act = jnp.einsum("gxcd,xdh->gxch", arrived, up_weight, preferred_element_type=jnp.float32)
    act_value, act_slope = gelu_pair(pre_act)
    activated = act_value.astype(jnp.bfloat16)
    produced = jnp.einsum(
        "gxch,xhd->gxcd", activated, down_weight, preferred_element_type=jnp.float32
    ).astype(jnp.bfloat16)
    gate_rows = gate_values[0]
    expert_mix = jnp.sum(gate_rows[:, :, None] * return_rows(produced), axis=1)
    layer_output = (attended_f + expert_mix).astype(jnp.bfloat16)
    upstream = cotangent[0].astype(jnp.float32)
    grad_out_rows = (
        (gate_rows[:, :, None] * upstream[:, None, :])
        .astype(jnp.bfloat16)
        .reshape(tok_rows * TOP, model_width)
    )
    grad_arrived = send_rows(grad_out_rows)
    grad_act = jnp.einsum(
        "gxcd,xhd->gxch", grad_arrived, down_weight, preferred_element_type=jnp.float32
    )
    grad_pre = (grad_act * act_slope).astype(jnp.bfloat16)
    down_local = jnp.einsum(
        "gxch,gxcd->xhd", activated, grad_arrived, preferred_element_type=jnp.float32
    )
    up_local = jnp.einsum("gxcd,gxch->xdh", arrived, grad_pre, preferred_element_type=jnp.float32)
    grad_normed = jnp.einsum(
        "gxch,xdh->gxcd", grad_pre, up_weight, preferred_element_type=jnp.float32
    ).astype(jnp.bfloat16)
    grad_unit = jnp.sum(return_rows(grad_normed), axis=1)
    grad_attended = upstream + inverse_rms * (
        grad_unit - unit_rows * jnp.mean(grad_unit * unit_rows, axis=-1, keepdims=True)
    )
    grad_attended = grad_attended.astype(jnp.bfloat16)
    grad_heads = lax.all_to_all(
        grad_attended, "seq", split_axis=1, concat_axis=0, tiled=True
    ).reshape(head_shape)
    grad_q, grad_k, grad_v = attention_backward(query_split, key_split, value_split, grad_heads)
    flat_shape = (head_shape[0], head_shape[1] * DH)
    grad_queries, grad_keys, grad_values = (
        lax.all_to_all(grad_q.reshape(flat_shape), "seq", split_axis=0, concat_axis=1, tiled=True),
        lax.all_to_all(
            grad_k.astype(jnp.bfloat16).reshape(flat_shape),
            "seq",
            split_axis=0,
            concat_axis=1,
            tiled=True,
        ),
        lax.all_to_all(
            grad_v.astype(jnp.bfloat16).reshape(flat_shape),
            "seq",
            split_axis=0,
            concat_axis=1,
            tiled=True,
        ),
    )
    grad_up, grad_down = (
        lax.psum_scatter(
            up_local.astype(jnp.bfloat16), ("dp", "seq"), scatter_dimension=1, tiled=True
        ).astype(jnp.float32),
        lax.psum_scatter(
            down_local.astype(jnp.bfloat16), ("dp", "seq"), scatter_dimension=2, tiled=True
        ).astype(jnp.float32),
    )
    return (
        layer_output[None],
        grad_queries[None],
        grad_keys[None],
        grad_values[None],
        grad_up,
        grad_down,
    )


def solution(mesh):
    in_specs = (
        P(("dp", "expert"), "seq", None),
        P(("dp", "expert"), "seq", None),
        P(("dp", "expert"), "seq", None),
        P(("dp", "expert"), "seq", None),
        P(("dp", "expert"), "seq", None),
        P("expert", None, None),
        P("expert", None, None),
        P(("dp", "expert"), "seq", None),
    )
    out_specs = (
        P(("dp", "expert"), "seq", None),
        P(("dp", "expert"), "seq", None),
        P(("dp", "expert"), "seq", None),
        P(("dp", "expert"), "seq", None),
        P("expert", ("dp", "seq"), None),
        P("expert", None, ("dp", "seq")),
    )
    return jax.shard_map(shards, mesh=mesh, in_specs=in_specs, out_specs=out_specs, check_vma=False)
```

profile of v0, /device:TPU:0, one launch (start us, length us, event | category | flops | bytes accessed | tf_op | source)
XLA Modules:
  0.0 253.7 jit_solution(7297019539599113075)
XLA Ops:
  7.2 1.2 all_to_all.104
  9.1 5.2 %all-to-all-start = ((bf16[128,4,256]{2,0,1:T(8,128)(2,1)}), bf16[128,4,256]{2,0,1:T(8,128)(2,1)S(1)}, u32[]{:S(2)}, u32[]{:S(2)}) async-start(bf16[128,4,256]{2,0,1:T(8,128)(2,1)} %copy.84), calls=%async_computation | async-start | bytes 524288 | tf_op jit(solution)/shard_map/all_to_all | solution.py:98
  17.1 2.6 %all-to-all-done = bf16[128,4,256]{2,0,1:T(8,128)(2,1)S(1)} async-done(((bf16[128,4,256]{2,0,1:T(8,128)(2,1)}), bf16[128,4,256]{2,0,1:T(8,128)(2,1)S(1)}, u32[]{:S(2)}, u32[]{:S(2)}) %all-to-all-start) | async-done | bytes 262176 | tf_op jit(solution)/shard_map/all_to_all | solution.py:98
  19.6 3.4 %all-to-all-start.1 = ((bf16[128,4,256]{2,0,1:T(8,128)(2,1)}), bf16[128,4,256]{2,0,1:T(8,128)(2,1)S(1)}, u32[]{:S(2)}, u32[]{:S(2)}) async-start(bf16[128,4,256]{2,0,1:T(8,128)(2,1)} %copy.85), calls=%async_computation.1 | async-start | bytes 524288 | tf_op jit(solution)/shard_map/all_to_all | solution.py:99
  23.1 1.2 reduce-window.6
  25.5 2.9 %all-to-all-done.1 = bf16[128,4,256]{2,0,1:T(8,128)(2,1)S(1)} async-done(((bf16[128,4,256]{2,0,1:T(8,128)(2,1)}), bf16[128,4,256]{2,0,1:T(8,128)(2,1)S(1)}, u32[]{:S(2)}, u32[]{:S(2)}) %all-to-all-start.1) | async-done | bytes 262176 | tf_op jit(solution)/shard_map/all_to_all | solution.py:99
  28.4 3.4 %all-to-all-start.2 = ((bf16[128,4,256]{2,0,1:T(8,128)(2,1)}), bf16[128,4,256]{2,0,1:T(8,128)(2,1)S(1)}, u32[]{:S(2)}, u32[]{:S(2)}) async-start(bf16[128,4,256]{2,0,1:T(8,128)(2,1)} %copy.88), calls=%async_computation.2 | async-start | bytes 524288 | tf_op jit(solution)/shard_map/all_to_all | solution.py:100
  32.2 4.9 %all-to-all-done.2 = bf16[128,4,256]{2,0,1:T(8,128)(2,1)S(1)} async-done(((bf16[128,4,256]{2,0,1:T(8,128)(2,1)}), bf16[128,4,256]{2,0,1:T(8,128)(2,1)S(1)}, u32[]{:S(2)}, u32[]{:S(2)}) %all-to-all-start.2) | async-done | bytes 262176 | tf_op jit(solution)/shard_map/all_to_all | solution.py:100
  37.2 2.2 fusion.119
  39.4 2.1 fusion.57
  42.7 3.4 %all-to-all-start.3 = ((bf16[4,128,256]{2,1,0:T(8,128)(2,1)}), bf16[4,128,256]{2,1,0:T(8,128)(2,1)S(1)}, u32[]{:S(2)}, u32[]{:S(2)}) async-start(bf16[4,128,256]{2,1,0:T(8,128)(2,1)} %all_to_all.113), calls=%async_computation.3 | async-start | bytes 524288 | tf_op jit(solution)/shard_map/all_to_all | solution.py:107
  46.1 5.3 %all-to-all-done.3 = bf16[4,128,256]{2,1,0:T(8,128)(2,1)S(1)} async-done(((bf16[4,128,256]{2,1,0:T(8,128)(2,1)}), bf16[4,128,256]{2,1,0:T(8,128)(2,1)S(1)}, u32[]{:S(2)}, u32[]{:S(2)}) %all-to-all-start.3) | async-done | bytes 262176 | tf_op jit(solution)/shard_map/all_to_all | solution.py:107
  52.5 1.4 convolution_convert_fusion.1
  53.9 4.9 %all-to-all-start.4 = ((bf16[4,96,1024]{2,1,0:T(8,128)(2,1)}), bf16[4,96,1024]{2,1,0:T(8,128)(2,1)}, u32[]{:S(2)}, u32[]{:S(2)}) async-start(bf16[4,96,1024]{2,1,0:T(8,128)(2,1)} %bitcast.12), calls=%async_computation.4 | async-start | bytes 1572864 | tf_op jit(solution)/shard_map/all_to_all | solution.py:120
  60.6 1.4 convolution_convert_fusion
  61.9 12.2 %all-to-all-done.4 = bf16[4,96,1024]{2,1,0:T(8,128)(2,1)} async-done(((bf16[4,96,1024]{2,1,0:T(8,128)(2,1)}), bf16[4,96,1024]{2,1,0:T(8,128)(2,1)}, u32[]{:S(2)}, u32[]{:S(2)}) %all-to-all-start.4) | async-done | bytes 786464 | tf_op jit(solution)/shard_map/all_to_all | solution.py:120
  74.2 3.5 %all-to-all-start.6 = ((bf16[4,96,1024]{2,1,0:T(8,128)(2,1)}), bf16[4,96,1024]{2,1,0:T(8,128)(2,1)S(1)}, u32[]{:S(2)}, u32[]{:S(2)}) async-start(bf16[4,96,1024]{2,1,0:T(8,128)(2,1)} %bitcast.28), calls=%async_computation.6 | async-start | bytes 1572864 | tf_op jit(solution)/shard_map/all_to_all | solution.py:120
  77.9 5.9 %fusion.8 = f32[4,96,2048]{2,1,0:T(8,128)} fusion(bf16[4,96,1024]{2,1,0:T(8,128)(2,1)} %all-to-all-done.4, bf16[1,1024,2048]{2,1,0:T(8,128)(2,1)} %param.13), kind=kOutput, calls=%fused_computation.13 | convolution fusion | flops 1610612736 | bytes 8126464 | tf_op jit(solution)/shard_map/gxcd,xdh->gxch/dot_general | solution.py:147
  83.8 11.0 %all-to-all-done.6 = bf16[4,96,1024]{2,1,0:T(8,128)(2,1)S(1)} async-done(((bf16[4,96,1024]{2,1,0:T(8,128)(2,1)}), bf16[4,96,1024]{2,1,0:T(8,128)(2,1)S(1)}, u32[]{:S(2)}, u32[]{:S(2)}) %all-to-all-start.6) | async-done | bytes 786464 | tf_op jit(solution)/shard_map/all_to_all | solution.py:120
  94.8 6.5 %fusion.11 = bf16[1,2048,1024]{2,1,0:T(8,128)(2,1)} fusion(bf16[4,96,1024]{2,1,0:T(8,128)(2,1)S(1)} %all-to-all-done.6, f32[4,96,2048]{2,1,0:T(8,128)} %fusion.8), kind=kOutput, calls=%fused_computation.16 | convolution fusion | flops 1619787776 | bytes 8126464 | tf_op jit(solution)/shard_map/gxch,gxcd->xhd/dot_general | solution.py:167
  101.2 20.6 %copy.127 = bf16[1,2048,1024]{1,0,2:T(2,128)(2,1)} copy(bf16[1,2048,1024]{2,1,0:T(8,128)(2,1)} %fusion.11) | data formatting | bytes 8388608
  121.8 8.0 %copy.161 = bf16[1024,1,2048]{2,0,1:T(8,128)(2,1)} copy(bf16[1024,1,2048]{2,1,0:T(2,128)(2,1)} %bitcast.179) | data formatting | bytes 8388608
  130.1 6.9 %fusion.21 = bf16[4,96,2048]{2,1,0:T(8,128)(2,1)S(1)} fusion(f32[4,96,2048]{2,1,0:T(8,128)} %fusion.8, bf16[4,96,1024]{2,1,0:T(8,128)(2,1)S(1)} %all-to-all-done.6, bf16[1,2048,1024]{2,1,0:T(8,128)(2,1)} %param.14), kind=kOutput, calls=%fused_computation.26 | convolution fusion | flops 1625554944 | bytes 9699328 | tf_op jit(solution)/shard_map/gxcd,xhd->gxch/dot_general | solution.py:163
  137.0 1.2 copy-done.6
  138.2 5.5 %fusion.10 = bf16[1,1024,2048]{2,1,0:T(8,128)(2,1)} fusion(bf16[4,96,1024]{2,1,0:T(8,128)(2,1)} %all-to-all-done.4, bf16[4,96,2048]{2,1,0:T(8,128)(2,1)S(1)} %fusion.21), kind=kOutput, calls=%fused_computation.15 | convolution fusion | flops 1612709888 | bytes 6553600 | tf_op jit(solution)/shard_map/gxcd,gxch->xdh/dot_general | solution.py:170
  143.7 1.4 copy-done.7
  145.1 4.9 %fusion.36 = bf16[4,96,1024]{2,1,0:T(8,128)(2,1)} fusion(bf16[4,96,2048]{2,1,0:T(8,128)(2,1)S(1)} %copy-done.7, bf16[1,1024,2048]{2,1,0:T(8,128)(2,1)} %param.13), kind=kOutput, calls=%fused_computation.37 | convolution fusion | flops 1611005952 | bytes 6553600 | tf_op jit(solution)/shard_map/gxch,xdh->gxcd/dot_general | solution.py:171
  150.0 3.5 %all-to-all-start.7 = ((bf16[4,96,1024]{2,1,0:T(8,128)(2,1)}), bf16[4,96,1024]{2,1,0:T(8,128)(2,1)S(1)}, u32[]{:S(2)}, u32[]{:S(2)}) async-start(bf16[4,96,1024]{2,1,0:T(8,128)(2,1)} %fusion.36), calls=%async_computation.7 | async-start | bytes 1572864 | tf_op jit(solution)/shard_map/all_to_all | solution.py:130
  153.5 6.1 %fusion.39 = bf16[4,96,1024]{2,1,0:T(8,128)(2,1)} fusion(bf16[1,2048,1024]{2,1,0:T(8,128)(2,1)} %param.14, f32[4,96,2048]{2,1,0:T(8,128)} %fusion.8), kind=kOutput, calls=%fused_computation.38 | convolution fusion | flops 1618083840 | bytes 8126464 | tf_op jit(solution)/shard_map/gxch,xhd->gxcd/dot_general | solution.py:150
  159.6 12.0 %all-to-all-done.7 = bf16[4,96,1024]{2,1,0:T(8,128)(2,1)S(1)} async-done(((bf16[4,96,1024]{2,1,0:T(8,128)(2,1)}), bf16[4,96,1024]{2,1,0:T(8,128)(2,1)S(1)}, u32[]{:S(2)}, u32[]{:S(2)}) %all-to-all-start.7) | async-done | bytes 786464 | tf_op jit(solution)/shard_map/all_to_all | solution.py:130
  171.6 4.2 %all-to-all-start.5 = ((bf16[4,96,1024]{2,1,0:T(8,128)(2,1)}), bf16[4,96,1024]{2,1,0:T(8,128)(2,1)}, u32[]{:S(2)}, u32[]{:S(2)}) async-start(bf16[4,96,1024]{2,1,0:T(8,128)(2,1)} %fusion.39), calls=%async_computation.5 | async-start | bytes 1572864 | tf_op jit(solution)/shard_map/all_to_all | solution.py:130
  178.3 16.9 %all-to-all-done.5 = bf16[4,96,1024]{2,1,0:T(8,128)(2,1)} async-done(((bf16[4,96,1024]{2,1,0:T(8,128)(2,1)}), bf16[4,96,1024]{2,1,0:T(8,128)(2,1)}, u32[]{:S(2)}, u32[]{:S(2)}) %all-to-all-start.5) | async-done | bytes 786464 | tf_op jit(solution)/shard_map/all_to_all | solution.py:130
  195.2 3.4 %all-to-all-start.8 = ((bf16[128,4,256]{2,0,1:T(8,128)(2,1)}), bf16[128,4,256]{2,0,1:T(8,128)(2,1)S(1)}, u32[]{:S(2)}, u32[]{:S(2)}) async-start(bf16[128,4,256]{2,0,1:T(8,128)(2,1)} %fusion.70), calls=%async_computation.8 | async-start | bytes 524288 | tf_op jit(solution)/shard_map/all_to_all | solution.py:179
  198.8 2.5 fusion.44
  201.3 2.7 %all-to-all-done.8 = bf16[128,4,256]{2,0,1:T(8,128)(2,1)S(1)} async-done(((bf16[128,4,256]{2,0,1:T(8,128)(2,1)}), bf16[128,4,256]{2,0,1:T(8,128)(2,1)S(1)}, u32[]{:S(2)}, u32[]{:S(2)}) %all-to-all-start.8) | async-done | bytes 262176 | tf_op jit(solution)/shard_map/all_to_all | solution.py:179
  204.2 2.5 fusion.58
  207.5 3.4 %all-to-all-start.11 = ((bf16[4,128,256]{1,2,0:T(8,128)(2,1)}), bf16[4,128,256]{1,2,0:T(8,128)(2,1)S(1)}, u32[]{:S(2)}, u32[]{:S(2)}) async-start(bf16[4,128,256]{1,2,0:T(8,128)(2,1)} %copy.120), calls=%async_computation.11 | async-start | bytes 524288 | tf_op jit(solution)/shard_map/all_to_all | solution.py:193
  211.4 4.1 %fusion.54 = bf16[512,2,128]{2,0,1:T(8,128)(2,1)} fusion(f32[2,512,512]{1,2,0:T(8,128)S(1)} %fusion.79, bf16[512,2,128]{2,1,0:T(2,128)(2,1)} %copy-done.4, f32[2,512,512]{1,2,0:T(8,128)} %get-tuple-element.58, f32[2,512]{1,0:T(2,128)S(1)} %get-tuple-element.57), kind=kOutput, calls=%fused_computation.49 | convolution fusion | flops 138020352 | bytes 4722688 | tf_op jit(solution)/shard_map/while/body/eval_jaxpr/hqk,khd->qhd/dot_general | solution.py:67
  215.5 1.2 copy.113
  217.6 1.5 all-to-all-done.11
  219.1 3.7 %all-to-all-start.9 = ((bf16[4,128,256]{2,1,0:T(8,128)(2,1)}), bf16[4,128,256]{2,1,0:T(8,128)(2,1)S(1)}, u32[]{:S(2)}, u32[]{:S(2)}) async-start(bf16[4,128,256]{2,1,0:T(8,128)(2,1)} %all_to_all.121), calls=%async_computation.9 | async-start | bytes 524288 | tf_op jit(solution)/shard_map/all_to_all | solution.py:185
  222.8 3.9 %fusion.51 = bf16[512,2,128]{2,0,1:T(8,128)(2,1)} fusion(f32[2,512,512]{1,2,0:T(8,128)S(1)} %fusion.79, bf16[512,2,128]{2,1,0:T(2,128)(2,1)S(1)} %copy-done.3, f32[2,512,512]{1,2,0:T(8,128)} %get-tuple-element.58, f32[2,512]{1,0:T(2,128)S(1)} %get-tuple-element.57), kind=kOutput, calls=%fused_computation.48 | convolution fusion | flops 138020352 | bytes 4722688 | tf_op jit(solution)/shard_map/while/body/eval_jaxpr/hqk,qhd->khd/dot_general | solution.py:70
  226.7 1.2 copy.116
  228.8 4.1 %all-to-all-start.10 = ((bf16[4,128,256]{2,1,0:T(8,128)(2,1)}), bf16[4,128,256]{2,1,0:T(8,128)(2,1)S(1)}, u32[]{:S(2)}, u32[]{:S(2)}) async-start(bf16[4,128,256]{2,1,0:T(8,128)(2,1)} %all_to_all.124), calls=%async_computation.10 | async-start | bytes 524288 | tf_op jit(solution)/shard_map/all_to_all | solution.py:186
  232.9 1.8 fusion.71
  236.6 3.5 %all-to-all-done.10 = bf16[4,128,256]{2,1,0:T(8,128)(2,1)S(1)} async-done(((bf16[4,128,256]{2,1,0:T(8,128)(2,1)}), bf16[4,128,256]{2,1,0:T(8,128)(2,1)S(1)}, u32[]{:S(2)}, u32[]{:S(2)}) %all-to-all-start.10) | async-done | bytes 262176 | tf_op jit(solution)/shard_map/all_to_all | solution.py:186
  241.2 1.7 reshape_bitcast_fusion
  244.7 2.1 convert_element_type.185
  (83 shorter events, 20.2 us)
Async XLA Ops:
  7.2 17.4 %copy-start = (bf16[1,128,1024]{2,1,0:T(8,128)(2,1)S(1)}, bf16[1,128,1024]{2,1,0:T(8,128)(2,1)}, u32[]{:S(2)}) copy-start(bf16[1,128,1024]{2,1,0:T(8,128)(2,1)} %param.10) | copy-start | bytes 786436
  9.1 10.5 %all-to-all-start = ((bf16[128,4,256]{2,0,1:T(8,128)(2,1)}), bf16[128,4,256]{2,0,1:T(8,128)(2,1)S(1)}, u32[]{:S(2)}, u32[]{:S(2)}) async-start(bf16[128,4,256]{2,0,1:T(8,128)(2,1)} %copy.84), calls=%async_computation | async-start | bytes 524288 | tf_op jit(solution)/shard_map/all_to_all | solution.py:98
  19.6 8.8 %all-to-all-start.1 = ((bf16[128,4,256]{2,0,1:T(8,128)(2,1)}), bf16[128,4,256]{2,0,1:T(8,128)(2,1)S(1)}, u32[]{:S(2)}, u32[]{:S(2)}) async-start(bf16[128,4,256]{2,0,1:T(8,128)(2,1)} %copy.85), calls=%async_computation.1 | async-start | bytes 524288 | tf_op jit(solution)/shard_map/all_to_all | solution.py:99
  28.4 8.8 %all-to-all-start.2 = ((bf16[128,4,256]{2,0,1:T(8,128)(2,1)}), bf16[128,4,256]{2,0,1:T(8,128)(2,1)S(1)}, u32[]{:S(2)}, u32[]{:S(2)}) async-start(bf16[128,4,256]{2,0,1:T(8,128)(2,1)} %copy.88), calls=%async_computation.2 | async-start | bytes 524288 | tf_op jit(solution)/shard_map/all_to_all | solution.py:100
  32.1 9.4 %copy-start.2 = (bf16[512,2,128]{2,1,0:T(2,128)(2,1)}, bf16[512,2,128]{2,1,0:T(2,128)(2,1)S(1)}, u32[]{:S(2)}) copy-start(bf16[512,2,128]{2,1,0:T(2,128)(2,1)S(1)} %squeeze.15) | copy-start | bytes 786436
  32.2 9.3 %copy-start.4 = (bf16[512,2,128]{2,1,0:T(2,128)(2,1)}, bf16[512,2,128]{2,1,0:T(2,128)(2,1)S(1)}, u32[]{:S(2)}) copy-start(bf16[512,2,128]{2,1,0:T(2,128)(2,1)S(1)} %reshape.259) | copy-start | bytes 786436
  42.7 8.8 %all-to-all-start.3 = ((bf16[4,128,256]{2,1,0:T(8,128)(2,1)}), bf16[4,128,256]{2,1,0:T(8,128)(2,1)S(1)}, u32[]{:S(2)}, u32[]{:S(2)}) async-start(bf16[4,128,256]{2,1,0:T(8,128)(2,1)} %all_to_all.113), calls=%async_computation.3 | async-start | bytes 524288 | tf_op jit(solution)/shard_map/all_to_all | solution.py:107
  51.8 6.9 %copy-start.5 = (f32[1,128,2]{1,2,0:T(2,128)S(1)}, f32[1,128,2]{1,2,0:T(2,128)}, u32[]{:S(2)}) copy-start(f32[1,128,2]{1,2,0:T(2,128)} %param.12) | copy-start | bytes 3076
  51.8 7.2 %copy-start.1 = (bf16[1,128,1024]{2,1,0:T(8,128)(2,1)S(1)}, bf16[1,128,1024]{2,1,0:T(8,128)(2,1)}, u32[]{:S(2)}) copy-start(bf16[1,128,1024]{2,1,0:T(8,128)(2,1)} %param.15) | copy-start | bytes 786436
  53.9 20.3 %all-to-all-start.4 = ((bf16[4,96,1024]{2,1,0:T(8,128)(2,1)}), bf16[4,96,1024]{2,1,0:T(8,128)(2,1)}, u32[]{:S(2)}, u32[]{:S(2)}) async-start(bf16[4,96,1024]{2,1,0:T(8,128)(2,1)} %bitcast.12), calls=%async_computation.4 | async-start | bytes 1572864 | tf_op jit(solution)/shard_map/all_to_all | solution.py:120
  74.2 20.6 %all-to-all-start.6 = ((bf16[4,96,1024]{2,1,0:T(8,128)(2,1)}), bf16[4,96,1024]{2,1,0:T(8,128)(2,1)S(1)}, u32[]{:S(2)}, u32[]{:S(2)}) async-start(bf16[4,96,1024]{2,1,0:T(8,128)(2,1)} %bitcast.28), calls=%async_computation.6 | async-start | bytes 1572864 | tf_op jit(solution)/shard_map/all_to_all | solution.py:120
  77.7 163.5 %reduce-scatter.7.cloned.1.call-start = ((), (), s32[]{:S(2)}) async-start(), calls=%async_computation.15 | async-start | bytes 4718592
  129.8 114.9 %reduce-scatter.5.cloned.1.call-start = ((), (), s32[]{:S(2)}) async-start(), calls=%async_computation.14 | async-start | bytes 4718592 | tf_op jit(solution)/shard_map/reduce_scatter | solution.py:202
  137.0 1.2 copy-start.6
  143.7 1.4 copy-start.7
  150.0 21.6 %all-to-all-start.7 = ((bf16[4,96,1024]{2,1,0:T(8,128)(2,1)}), bf16[4,96,1024]{2,1,0:T(8,128)(2,1)S(1)}, u32[]{:S(2)}, u32[]{:S(2)}) async-start(bf16[4,96,1024]{2,1,0:T(8,128)(2,1)} %fusion.36), calls=%async_computation.7 | async-start | bytes 1572864 | tf_op jit(solution)/shard_map/all_to_all | solution.py:130
  171.6 23.6 %all-to-all-start.5 = ((bf16[4,96,1024]{2,1,0:T(8,128)(2,1)}), bf16[4,96,1024]{2,1,0:T(8,128)(2,1)}, u32[]{:S(2)}, u32[]{:S(2)}) async-start(bf16[4,96,1024]{2,1,0:T(8,128)(2,1)} %fusion.39), calls=%async_computation.5 | async-start | bytes 1572864 | tf_op jit(solution)/shard_map/all_to_all | solution.py:130
  195.2 8.8 %all-to-all-start.8 = ((bf16[128,4,256]{2,0,1:T(8,128)(2,1)}), bf16[128,4,256]{2,0,1:T(8,128)(2,1)S(1)}, u32[]{:S(2)}, u32[]{:S(2)}) async-start(bf16[128,4,256]{2,0,1:T(8,128)(2,1)} %fusion.70), calls=%async_computation.8 | async-start | bytes 524288 | tf_op jit(solution)/shard_map/all_to_all | solution.py:179
  207.5 11.5 %all-to-all-start.11 = ((bf16[4,128,256]{1,2,0:T(8,128)(2,1)}), bf16[4,128,256]{1,2,0:T(8,128)(2,1)S(1)}, u32[]{:S(2)}, u32[]{:S(2)}) async-start(bf16[4,128,256]{1,2,0:T(8,128)(2,1)} %copy.120), calls=%async_computation.11 | async-start | bytes 524288 | tf_op jit(solution)/shard_map/all_to_all | solution.py:193
  211.4 11.4 %copy-start.3 = (bf16[512,2,128]{2,1,0:T(2,128)(2,1)S(1)}, bf16[512,2,128]{2,1,0:T(2,128)(2,1)}, u32[]{:S(2)}) copy-start(bf16[512,2,128]{2,1,0:T(2,128)(2,1)} %copy-done.2) | copy-start | bytes 786436
  219.1 9.7 %all-to-all-start.9 = ((bf16[4,128,256]{2,1,0:T(8,128)(2,1)}), bf16[4,128,256]{2,1,0:T(8,128)(2,1)S(1)}, u32[]{:S(2)}, u32[]{:S(2)}) async-start(bf16[4,128,256]{2,1,0:T(8,128)(2,1)} %all_to_all.121), calls=%async_computation.9 | async-start | bytes 524288 | tf_op jit(solution)/shard_map/all_to_all | solution.py:185
  228.8 11.4 %all-to-all-start.10 = ((bf16[4,128,256]{2,1,0:T(8,128)(2,1)}), bf16[4,128,256]{2,1,0:T(8,128)(2,1)S(1)}, u32[]{:S(2)}, u32[]{:S(2)}) async-start(bf16[4,128,256]{2,1,0:T(8,128)(2,1)} %all_to_all.124), calls=%async_computation.10 | async-start | bytes 524288 | tf_op jit(solution)/shard_map/all_to_all | solution.py:186
Sparse Core Ops, SparseCore 0:
  129.9 49.2 reduce-scatter.6
  183.0 58.2 reduce-scatter.4
where the time goes:
time: 256 us; the launch traced here: 254 us
  waiting for transfers between devices  75.5 us (29%)
  matrix products  56.7 us (22%)
  local copies, waits for them, and re-layouts  52.6 us (21%)
  starting transfers between devices  46.5 us (18%)
  between operations  14.5 us (6%)
  other arithmetic  7.76 us (3%)
    unnamed x26, local copies, waits for them, and re-layouts  37.3 us
    all_to_all x2, waiting for transfers between devices, return_rows(): lax.all_to_all(results.reshape(owners, local_experts * capacity, model_wi...  29 us
    all_to_all x2, waiting for transfers between devices, send_rows(): lax.all_to_all(packed.reshape(owners, local_experts * capacity, model_wid...  23.2 us
    all_to_all x2, starting transfers between devices, send_rows(): lax.all_to_all(packed.reshape(owners, local_experts * capacity, model_wid...  8.36 us
    all_to_all x2, starting transfers between devices, return_rows(): lax.all_to_all(results.reshape(owners, local_experts * capacity, model_wi...  7.69 us
    dot_general x1, matrix products, shards(): jnp.einsum('gxcd,xhd->gxch', grad_arrived, down_weight, preferred_element...  6.88 us
    dot_general x1, matrix products, shards(): jnp.einsum('gxch,gxcd->xhd', activated, grad_arrived, preferred_element_t...  6.48 us
    dot_general x1, matrix products, shards(): jnp.einsum('gxch,xhd->gxcd', activated, down_weight, preferred_element_ty...  6.08 us
  transfers between devices with their start and end apart: 14, of which 11 were waited for; matrix products, arithmetic and copies ran while one was open for 25% of the time, Pallas kernels for 0%

commit v1 on v0

v1 whole, which is shorter than its diff:
```python
import functools
import math

import jax
import jax.numpy as jnp
from jax import lax
from jax.experimental import pallas as pl
from jax.experimental.pallas import tpu as pltpu
from jax.sharding import PartitionSpec as P

DH = 128
TOP = 2
EPSILON = 1e-06
GELU_COEF = math.sqrt(2.0 / math.pi)
MESH = pl.DeviceIdType.MESH
F32 = jnp.float32
BF16 = jnp.bfloat16
VMEM_LIMIT = 52 * 1024 * 1024


def gelu_pair(inputs):
    square = inputs * inputs
    hyper = jnp.tanh(GELU_COEF * inputs * (1.0 + 0.044715 * square))
    half = 0.5 * (1.0 + hyper)
    result = inputs * half
    slope = half + 0.5 * inputs * (1.0 - hyper * hyper) * GELU_COEF * (
        1.0 + 3.0 * 0.044715 * square
    )
    return result, slope


def dot_nn(a, b):
    return jnp.dot(a, b, preferred_element_type=F32)


def dot_nt(a, b):
    return lax.dot_general(a, b, (((1,), (1,)), ((), ())), preferred_element_type=F32)


def dot_tn(a, b):
    return lax.dot_general(a, b, (((0,), (0,)), ((), ())), preferred_element_type=F32)


def greet(axes):
    barrier = pltpu.get_barrier_semaphore()
    total = 0
    for axis in axes:
        size = lax.axis_size(axis)
        me = lax.axis_index(axis)
        for step in range(1, size):
            peer = lax.rem(me + step, size)
            pl.semaphore_signal(barrier, inc=1, device_id={axis: peer}, device_id_type=MESH)
            total += 1
    pl.semaphore_wait(barrier, total)


def remote(src, dst, send, recv, axis, peer):
    return pltpu.make_async_remote_copy(
        src_ref=src,
        dst_ref=dst,
        send_sem=send,
        recv_sem=recv,
        device_id={axis: peer},
        device_id_type=MESH,
    )


def split_cols(src, dst, send, recv, me, size):
    rows = src.shape[0]
    width = src.shape[1] // size
    copies = []
    for step in range(1, size):
        peer = lax.rem(me + step, size)
        copy = remote(
            src.at[:, pl.ds(pl.multiple_of(peer * width, width), width)],
            dst.at[pl.ds(pl.multiple_of(me * rows, rows), rows), :],
            send.at[step],
            recv.at[step],
            "seq",
            peer,
        )
        copy.start()
        copies.append(copy)
    own = src[:, pl.ds(pl.multiple_of(me * width, width), width)]
    dst[pl.ds(pl.multiple_of(me * rows, rows), rows), :] = own
    return copies


def join_block(src, dst, send, recv, me, size, step):
    rows = dst.shape[0]
    width = src.shape[1]
    peer = lax.rem(me + step, size)
    copy = remote(
        src.at[pl.ds(pl.multiple_of(peer * rows, rows), rows), :],
        dst.at[:, pl.ds(pl.multiple_of(me * width, width), width)],
        send.at[step],
        recv.at[step],
        "seq",
        peer,
    )
    copy.start()
    return copy


def join_rows(src, dst, send, recv, me, size):
    rows = dst.shape[0]
    width = src.shape[1]
    copies = [join_block(src, dst, send, recv, me, size, step) for step in range(1, size)]
    own = src[pl.ds(pl.multiple_of(me * rows, rows), rows), :]
    dst[:, pl.ds(pl.multiple_of(me * width, width), width)] = own
    return copies


def swap_slots(src, dst, send, recv, me, size):
    cap = src.shape[0] // size
    copies = []
    for step in range(1, size):
        peer = lax.rem(me + step, size)
        copy = remote(
            src.at[pl.ds(pl.multiple_of(peer * cap, cap), cap), :],
            dst.at[pl.ds(pl.multiple_of(me * cap, cap), cap), :],
            send.at[step],
            recv.at[step],
            "expert",
            peer,
        )
        copy.start()
        copies.append(copy)
    mine = pl.ds(pl.multiple_of(me * cap, cap), cap)
    dst[mine, :] = src[mine, :]
    return copies


def wait_all(copies):
    for copy in copies:
        copy.wait()


def softmax_rows(query, key):
    scores = dot_nt(query, key) * (1.0 / math.sqrt(DH))
    exponent = jnp.exp(scores - jnp.max(scores, axis=-1, keepdims=True))
    return exponent / jnp.sum(exponent, axis=-1, keepdims=True)


def forward_kernel(
    experts, cap,
    q_ref, k_ref, v_ref, routes_ref, gates_ref, cot_ref,
    qh_ref, kh_ref, vh_ref, att_ref, place_ref, grad_ref,
    packed, heads, seq_send, seq_recv, exp_send, exp_recv,
):
    n_seq = lax.axis_size("seq")
    n_exp = lax.axis_size("expert")
    me_seq = lax.axis_index("seq")
    me_exp = lax.axis_index("expert")
    rows = q_ref.shape[0]
    slots = experts * cap
    greet(("seq", "expert"))
    seq_copies = []
    for number, (src, dst) in enumerate(((q_ref, qh_ref), (k_ref, kh_ref), (v_ref, vh_ref))):
        seq_copies += split_cols(
            src, dst, seq_send.at[number], seq_recv.at[number], me_seq, n_seq
        )

    expert_ids = lax.broadcasted_iota(jnp.int32, (rows, experts), 1)
    hits = [
        jnp.where(routes_ref[:, j : j + 1] == expert_ids, 1.0, 0.0).astype(F32)
        for j in range(TOP)
    ]
    earlier = lax.broadcasted_iota(jnp.int32, (rows, rows), 1) < lax.broadcasted_iota(
        jnp.int32, (rows, rows), 0
    )
    rank = dot_nn(
        jnp.where(earlier, 1.0, 0.0).astype(BF16), (hits[0] + hits[1]).astype(BF16)
    )
    base = rank + (expert_ids * cap).astype(F32)
    slot_ids = lax.broadcasted_iota(jnp.int32, (rows, slots), 1).astype(F32)
    cot = cot_ref[...].astype(F32)
    total = None
    for j in range(TOP):
        slot = jnp.sum(hits[j] * base, axis=1, keepdims=True)
        placer = jnp.where(slot_ids == slot, 1.0, 0.0).astype(BF16)
        place_ref[j] = placer
        dout = (gates_ref[:, j : j + 1] * cot).astype(BF16)
        part = dot_tn(placer, dout)
        total = part if total is None else total + part
    packed[...] = total.astype(BF16)
    exp_copies = swap_slots(packed, grad_ref, exp_send, exp_recv, me_exp, n_exp)

    wait_all(seq_copies)
    width = heads.shape[1]
    back = []
    for step in [*range(1, n_seq), 0]:
        peer = lax.rem(me_seq + step, n_seq)
        block = pl.ds(pl.multiple_of(peer * rows, rows), rows)
        for head in range(width // DH):
            cols = slice(head * DH, (head + 1) * DH)
            probs = softmax_rows(qh_ref[block, cols], kh_ref[:, cols]).astype(BF16)
            heads[block, cols] = dot_nn(probs, vh_ref[:, cols]).astype(BF16)
        if step > 0:
            back.append(
                join_block(heads, att_ref, seq_send.at[3], seq_recv.at[3], me_seq, n_seq, step)
            )
        else:
            att_ref[:, pl.ds(pl.multiple_of(me_seq * width, width), width)] = heads[block, :]
    wait_all(back)
    wait_all(exp_copies)


def unit_of(att):
    att_f = att.astype(F32)
    inverse = lax.rsqrt(jnp.mean(att_f * att_f, axis=-1, keepdims=True) + EPSILON)
    return att_f, inverse, att_f * inverse


def expert_kernel(
    chunk,
    att_ref, place_ref, grad_ref, up_hbm, down_hbm,
    out_ref, dnorm_ref, gw_ref,
    packed, rows_in, up, down, dact, act, dpre, rows_t, grad_t,
    exp_send, exp_recv, load_sem,
):
    n_exp = lax.axis_size("expert")
    me_exp = lax.axis_index("expert")
    load_up = pltpu.make_async_copy(up_hbm, up, load_sem.at[0])
    load_down = pltpu.make_async_copy(down_hbm, down, load_sem.at[1])
    load_down.start()
    load_up.start()
    _, _, unit = unit_of(att_ref[...])
    placer = place_ref[0] + place_ref[1]
    packed[...] = dot_tn(placer, unit.astype(BF16)).astype(BF16)
    greet(("expert",))
    copies = swap_slots(packed, rows_in, exp_send, exp_recv, me_exp, n_exp)
    grad_t[...] = grad_ref[...].T
    load_down.wait()
    hidden = up.shape[1]
    model = up.shape[0]

    @pl.loop(0, hidden // chunk)
    def _(c):
        cols = pl.ds(pl.multiple_of(c * chunk, chunk), chunk)
        dact[:, cols] = dot_nt(grad_ref[...], down[cols, :])

    load_up.wait()
    wait_all(copies)

    @pl.loop(0, hidden // chunk)
    def _(c):
        cols = pl.ds(pl.multiple_of(c * chunk, chunk), chunk)
        value, slope = gelu_pair(dot_nn(rows_in[...], up[:, cols]))
        act[:, cols] = value.astype(BF16)
        dpre[:, cols] = (dact[:, cols] * slope).astype(BF16)

    @pl.loop(0, model // 256)
    def _(c):
        cols = pl.ds(pl.multiple_of(c * 256, 256), 256)
        dnorm_ref[:, cols] = dot_nt(dpre[...], up[cols, :]).astype(BF16)
        out_ref[:, cols] = dot_nn(act[...], down[:, cols]).astype(BF16)

    rows_t[...] = rows_in[...].T

    @pl.loop(0, hidden // chunk)
    def _(c):
        cols = pl.ds(pl.multiple_of(c * chunk, chunk), chunk)
        later = pl.ds(pl.multiple_of(hidden + c * chunk, chunk), chunk)
        gw_ref[:, cols] = dot_nn(rows_t[...], dpre[:, cols]).astype(BF16)
        gw_ref[:, later] = dot_nn(grad_t[...], act[:, cols]).astype(BF16)


def backward_kernel(
    out_ref, dnorm_ref, place_ref, gates_ref, cot_ref, att_ref, qh_ref, kh_ref, vh_ref,
    layer_ref, gq_ref, gk_ref, gv_ref,
    ret_out, ret_dnorm, datt, dheads, probs, gqh, gkh, gvh,
    seq_send, seq_recv, exp_send, exp_recv,
):
    n_seq = lax.axis_size("seq")
    n_exp = lax.axis_size("expert")
    me_seq = lax.axis_index("seq")
    me_exp = lax.axis_index("expert")
    greet(("seq", "expert"))
    dnorm_copies = swap_slots(
        dnorm_ref, ret_dnorm, exp_send.at[0], exp_recv.at[0], me_exp, n_exp
    )
    out_copies = swap_slots(out_ref, ret_out, exp_send.at[1], exp_recv.at[1], me_exp, n_exp)
    width = qh_ref.shape[1]
    for head in range(width // DH):
        cols = slice(head * DH, (head + 1) * DH)
        probs[head] = softmax_rows(qh_ref[:, cols], kh_ref[:, cols])
    att_f, inverse, unit = unit_of(att_ref[...])
    cot = cot_ref[...].astype(F32)
    wait_all(dnorm_copies)
    dunit = dot_nn(place_ref[0] + place_ref[1], ret_dnorm[...])
    datt[...] = (
        cot + inverse * (dunit - unit * jnp.mean(dunit * unit, axis=-1, keepdims=True))
    ).astype(BF16)
    wait_all(split_cols(datt, dheads, seq_send.at[0], seq_recv.at[0], me_seq, n_seq))
    scaling = 1.0 / math.sqrt(DH)
    for head in range(width // DH):
        cols = slice(head * DH, (head + 1) * DH)
        prob = probs[head]
        dhead = dheads[:, cols]
        gvh[:, cols] = dot_tn(prob.astype(BF16), dhead).astype(BF16)
        dprobs = dot_nt(dhead, vh_ref[:, cols])
        delta = jnp.sum(prob * dprobs, axis=-1, keepdims=True)
        dscores = (prob * (dprobs - delta) * scaling).astype(BF16)
        gkh[:, cols] = dot_tn(dscores, qh_ref[:, cols]).astype(BF16)
        gqh[:, cols] = dot_nn(dscores, kh_ref[:, cols]).astype(BF16)
    back = []
    for number, (src, dst) in enumerate(((gvh, gv_ref), (gkh, gk_ref), (gqh, gq_ref)), 1):
        back += join_rows(src, dst, seq_send.at[number], seq_recv.at[number], me_seq, n_seq)
    wait_all(out_copies)
    mixed = att_f
    mix = None
    for j in range(TOP):
        part = gates_ref[:, j : j + 1] * dot_nn(place_ref[j], ret_out[...])
        mix = part if mix is None else mix + part
    layer_ref[...] = (mixed + mix).astype(BF16)
    wait_all(back)


def shards(
    query_input, key_input, value_input, routes, gate_values, up_weight, down_weight, cotangent
):
    rows, model = query_input.shape[1:]
    n_seq = lax.axis_size("seq")
    n_exp = lax.axis_size("expert")
    hidden = up_weight.shape[2]
    experts = up_weight.shape[0] * n_exp
    cap = rows * TOP * 3 // (2 * experts)
    cap = -(-cap // 16) * 16
    slots = experts * cap
    width = model // n_seq
    tokens = rows * n_seq
    vmem = pl.BlockSpec(memory_space=pltpu.VMEM)
    hbm = pl.BlockSpec(memory_space=pl.ANY)
    dma = pltpu.SemaphoreType.DMA

    def shape(*dims, dtype=BF16):
        return jax.ShapeDtypeStruct(dims, dtype)

    def params(number):
        return pltpu.CompilerParams(
            collective_id=number, has_side_effects=True, vmem_limit_bytes=VMEM_LIMIT
        )

    gates = gate_values[0]
    cot = cotangent[0]
    qh, kh, vh, attended, placers, grad_in = pl.pallas_call(
        functools.partial(forward_kernel, experts, cap),
        name="attention_forward",
        out_shape=[shape(tokens, width)] * 3
        + [shape(rows, model), shape(TOP, rows, slots), shape(slots, model)],
        in_specs=[vmem] * 6,
        out_specs=[vmem] * 6,
        scratch_shapes=[
            pltpu.VMEM((slots, model), BF16),
            pltpu.VMEM((tokens, width), BF16),
            dma((4, n_seq)),
            dma((4, n_seq)),
            dma((n_exp,)),
            dma((n_exp,)),
        ],
        compiler_params=params(0),
        cost_estimate=pl.CostEstimate(
            flops=4 * tokens * tokens * width, bytes_accessed=8 * rows * model,
            transcendentals=0,
        ),
    )(query_input[0], key_input[0], value_input[0], routes[0], gates, cot)
    produced, dnormed, weight_grads = pl.pallas_call(
        functools.partial(expert_kernel, 512),
        name="expert_block",
        out_shape=[shape(slots, model), shape(slots, model), shape(model, 2 * hidden)],
        in_specs=[vmem] * 3 + [hbm] * 2,
        out_specs=[vmem] * 3,
        scratch_shapes=[
            pltpu.VMEM((slots, model), BF16),
            pltpu.VMEM((slots, model), BF16),
            pltpu.VMEM((model, hidden), BF16),
            pltpu.VMEM((hidden, model), BF16),
            pltpu.VMEM((slots, hidden), F32),
            pltpu.VMEM((slots, hidden), BF16),
            pltpu.VMEM((slots, hidden), BF16),
            pltpu.VMEM((model, slots), BF16),
            pltpu.VMEM((model, slots), BF16),
            dma((n_exp,)),
            dma((n_exp,)),
            dma((2,)),
        ],
        compiler_params=params(1),
        cost_estimate=pl.CostEstimate(
            flops=12 * slots * model * hidden, bytes_accessed=8 * model * hidden,
            transcendentals=0,
        ),
    )(attended, placers, grad_in, up_weight[0], down_weight[0])
    halves = lax.psum_scatter(weight_grads, "dp", scatter_dimension=0, tiled=True)
    summed = lax.psum_scatter(halves, "seq", scatter_dimension=0, tiled=True)
    layer, grad_q, grad_k, grad_v = pl.pallas_call(
        backward_kernel,
        name="attention_backward",
        out_shape=[shape(rows, model)] * 4,
        in_specs=[vmem] * 9,
        out_specs=[vmem] * 4,
        scratch_shapes=[
            pltpu.VMEM((slots, model), BF16),
            pltpu.VMEM((slots, model), BF16),
            pltpu.VMEM((rows, model), BF16),
            pltpu.VMEM((tokens, width), BF16),
            pltpu.VMEM((width // DH, tokens, tokens), F32),
            pltpu.VMEM((tokens, width), BF16),
            pltpu.VMEM((tokens, width), BF16),
            pltpu.VMEM((tokens, width), BF16),
            dma((4, n_seq)),
            dma((4, n_seq)),
            dma((2, n_exp)),
            dma((2, n_exp)),
        ],
        compiler_params=params(2),
        cost_estimate=pl.CostEstimate(
            flops=60_000_000_000, bytes_accessed=100_000_000, transcendentals=0
        ),
    )(produced, dnormed, placers, gates, cot, attended, qh, kh, vh)
    summed = summed.astype(F32)
    return (
        layer[None],
        grad_q[None],
        grad_k[None],
        grad_v[None],
        summed[None, :, :hidden],
        summed[:, hidden:].T[None],
    )


def solution(mesh):
    tokens = P(("dp", "expert"), "seq", None)
    weights = P("expert", None, None)
    in_specs = (tokens,) * 5 + (weights, weights, tokens)
    out_specs = (tokens,) * 4 + (P("expert", ("dp", "seq"), None), P("expert", None, ("dp", "seq")))
    return jax.shard_map(shards, mesh=mesh, in_specs=in_specs, out_specs=out_specs, check_vma=False)
```

time: 256 us -> 176 us (0.69)
  the two profiles are of different devices: /device:TPU:0 before, /device:TPU:24 now
where the time goes in v1:
time: 176 us; the launch traced here: 174 us
  Pallas kernels  108 us (61%)
  waiting for transfers between devices  37.6 us (21%)
  between operations  14.1 us (8%)
  local copies, waits for them, and re-layouts  12.6 us (7%)
    pallas_call x1, Pallas kernels, shards(): pl.pallas_call(backward_kernel, name='attention_backward', out_shape=[sha...  47.1 us
    pallas_call x1, Pallas kernels, shards(): pl.pallas_call(functools.partial(expert_kernel, 512), name='expert_block'...  37.5 us
    pallas_call x1, Pallas kernels, shards(): pl.pallas_call(functools.partial(forward_kernel, experts, cap), name='att...  23.5 us
    reduce_scatter x1, waiting for transfers between devices, shards(): summed = lax.psum_scatter(halves, 'seq', scatter_dimension=0, tiled=True)  20.2 us
    reduce_scatter x1, waiting for transfers between devices, shards(): lax.psum_scatter(weight_grads, 'dp', scatter_dimension=0, tiled=True)  17.4 us
    unnamed x23, local copies, waits for them, and re-layouts  11.4 us
  transfers between devices with their start and end apart: 2, of which 2 were waited for; matrix products, arithmetic and copies ran while one was open for 0% of the time, Pallas kernels for 27%

profile of v1, /device:TPU:24, one launch (start us, length us, event | category | flops | bytes accessed | tf_op | source)
XLA Modules:
  0.0 173.9 jit_solution(11798824828056633788)
XLA Ops:
  7.2 0.0 reduce-scatter.3.cloned.1.call-start
  7.2 0.8 copy.14
  8.0 0.8 copy.15
  8.8 0.0 copy-start
  8.8 0.9 copy-done
  9.7 0.0 copy-start.1
  9.7 0.9 copy-done.1
  10.7 23.5 %attention_forward.1 = (bf16[512,256]{1,0:T(8,128)(2,1)S(1)}, bf16[512,256]{1,0:T(8,128)(2,1)S(1)}, bf16[512,256]{1,0:T(8,128)(2,1)S(1)}, bf16[128,1024]{1,0:T(8...) custom-call(bf16[128,1024]{1,0:T(8,128)(2,1)S(1)} %bitcast.25, ...), custom_call_target="tpu_custom_call" | custom-call | flops 268435456 | bytes 1048576 | tf_op jit(solution)/shard_map/attention_forward/pallas_call | solution.py:347
  34.2 0.0 copy-start.3
  34.2 0.7 copy-done.3
  34.9 0.0 copy-start.4
  34.9 0.7 copy-done.4
  35.6 0.0 copy-start.5
  35.6 0.7 copy-done.5
  36.3 37.5 %expert_block.1 = (bf16[384,1024]{1,0:T(8,128)(2,1)S(1)}, bf16[384,1024]{1,0:T(8,128)(2,1)S(1)}, bf16[1024,4096]{1,0:T(8,128)(2,1)}) custom-call(bf16[128,1024]{1,0:T(8,128)(2,1)S(1)} %get-tuple-element.19.att_ref, bf16[2,128,384]{2,1,0:T(8,128)(2,1)S(1)} %get-tuple-element.20.place_ref, bf16[384,1024]{1,0:T(8,128)(2,1)} %get-tuple-element.21.grad_ref, ...), custom_call_target="tpu_custom_call" | custom-call | flops 9663676416 | bytes 16777216 | tf_op jit(solution)/shard_map/expert_block/pallas_call | solution.py:368
  73.9 0.0 copy-start.6
  73.9 0.9 copy-done.6
  74.7 0.0 copy-start.7
  74.7 0.0 reduce-scatter.3.cloned.1.call-update
  74.8 0.9 copy-done.7
  75.6 0.0 copy-start.2
  75.6 0.0 reduce-scatter.5.cloned.1.call-start
  75.6 17.4 %reduce-scatter.3.cloned.1.call-done = bf16[512,4096]{1,0:T(8,128)(2,1)} async-done(((bf16[1024,4096]{1,0:T(8,128)(2,1)}), bf16[512,4096]{1,0:T(8,128)(2,1)}) %reduce-scatter.3.cloned.1.call-update) | async-done | bytes 4194320 | tf_op jit(solution)/shard_map/reduce_scatter | solution.py:394
  93.0 0.0 reduce-scatter.5.cloned.1.call-update
  93.1 0.0 copy-done.2
  93.1 47.1 %attention_backward.1 = (bf16[128,1024]{1,0:T(8,128)(2,1)S(1)}, bf16[128,1024]{1,0:T(8,128)(2,1)S(1)}, bf16[128,1024]{1,0:T(8,128)(2,1)S(1)}, bf16[128,1024]{1,0:T(8,128)(2,1)S(1)}) custom-call(bf16[384,1024]{1,0:T(8,128)(2,1)} %copy-done.6, bf16[384,1024]{1,0:T(8,128)(2,1)} %copy-done.7, bf16[2,128,384]{2,1,0:T(8,128)(2,1)S(1)} %get-tuple-element.20.place_ref, ...), custom_call_target="tpu_custom_call" | custom-call | flops 60000002048 | bytes 100000000 | tf_op jit(solution)/shard_map/attention_backward/pallas_call | solution.py:396
  140.2 20.2 %reduce-scatter.5.cloned.1.call-done = bf16[128,4096]{1,0:T(8,128)(2,1)} async-done(((bf16[512,4096]{1,0:T(8,128)(2,1)}), bf16[128,4096]{1,0:T(8,128)(2,1)}) %reduce-scatter.5.cloned.1.call-update) | async-done | bytes 1048592 | tf_op jit(solution)/shard_map/reduce_scatter | solution.py:395
  160.3 1.4 convert_element_type.3
  161.7 1.2 slice_bitcast_fusion
  162.9 1.3 copy.16
  164.2 0.7 copy.21
  164.9 0.7 copy.22
  165.6 0.7 copy.23
  166.3 0.7 copy.24
Async XLA Ops:
  7.2 85.9 %reduce-scatter.3.cloned.1.call-start = ((), (), s32[]{:S(2)}) async-start(), calls=%async_computation.2 | async-start | bytes 12582912 | tf_op jit(solution)/shard_map/reduce_scatter | solution.py:394
  8.8 0.9 copy-start
  9.7 0.9 copy-start.1
  34.2 0.7 copy-start.3
  34.9 0.7 copy-start.4
  35.6 0.7 copy-start.5
  73.9 0.9 copy-start.6
  74.7 0.9 copy-start.7
  75.6 17.5 %copy-start.2 = (bf16[1,128,1024]{2,1,0:T(8,128)(2,1)S(1)}, bf16[1,128,1024]{2,1,0:T(8,128)(2,1)}, u32[]{:S(2)}) copy-start(bf16[1,128,1024]{2,1,0:T(8,128)(2,1)} %param.15) | copy-start | bytes 786436
  75.6 84.7 %reduce-scatter.5.cloned.1.call-start = ((), (), s32[]{:S(2)}) async-start(), calls=%async_computation.3 | async-start | bytes 5242880 | tf_op jit(solution)/shard_map/reduce_scatter | solution.py:395
Sparse Core Ops, SparseCore 0:
  74.9 18.1 reduce-scatter.2
  96.3 63.9 reduce-scatter.4

commit v2 on v1

v2 whole, which is shorter than its diff:
```python
import functools
import math

import jax
import jax.numpy as jnp
from jax import lax
from jax.experimental import pallas as pl
from jax.experimental.pallas import tpu as pltpu
from jax.sharding import PartitionSpec as P

DH = 128
TOP = 2
EPSILON = 1e-06
GELU_COEF = math.sqrt(2.0 / math.pi)
MESH = pl.DeviceIdType.MESH
F32 = jnp.float32
BF16 = jnp.bfloat16
VMEM_LIMIT = 60 * 1024 * 1024


def gelu_pair(inputs):
    square = inputs * inputs
    hyper = jnp.tanh(GELU_COEF * inputs * (1.0 + 0.044715 * square))
    half = 0.5 * (1.0 + hyper)
    result = inputs * half
    slope = half + 0.5 * inputs * (1.0 - hyper * hyper) * GELU_COEF * (
        1.0 + 3.0 * 0.044715 * square
    )
    return result, slope


def dot_nn(a, b):
    return jnp.dot(a, b, preferred_element_type=F32)


def dot_nt(a, b):
    return lax.dot_general(a, b, (((1,), (1,)), ((), ())), preferred_element_type=F32)


def dot_tn(a, b):
    return lax.dot_general(a, b, (((0,), (0,)), ((), ())), preferred_element_type=F32)


def greet(axes):
    barrier = pltpu.get_barrier_semaphore()
    total = 0
    for axis in axes:
        size = lax.axis_size(axis)
        me = lax.axis_index(axis)
        for step in range(1, size):
            peer = lax.rem(me + step, size)
            pl.semaphore_signal(barrier, inc=1, device_id={axis: peer}, device_id_type=MESH)
            total += 1
    pl.semaphore_wait(barrier, total)


def remote(src, dst, send, recv, axis, peer):
    return pltpu.make_async_remote_copy(
        src_ref=src,
        dst_ref=dst,
        send_sem=send,
        recv_sem=recv,
        device_id={axis: peer},
        device_id_type=MESH,
    )


def rows_of(index, count):
    return pl.ds(pl.multiple_of(index * count, count), count)


def split_cols(src, dst, send, recv, me, size, own_sem):
    rows = src.shape[0]
    width = src.shape[1] // size
    copies = []
    for step in range(1, size):
        peer = lax.rem(me + step, size)
        copy = remote(
            src.at[:, rows_of(peer, width)],
            dst.at[rows_of(me, rows), :],
            send.at[step],
            recv.at[step],
            "seq",
            peer,
        )
        copy.start()
        copies.append(copy)
    own = pltpu.make_async_copy(src.at[:, rows_of(me, width)], dst.at[rows_of(me, rows), :], own_sem)
    own.start()
    return copies, own


def join_block(src, dst, send, recv, me, size, step):
    rows = dst.shape[0]
    width = src.shape[1]
    peer = lax.rem(me + step, size)
    copy = remote(
        src.at[rows_of(peer, rows), :],
        dst.at[:, rows_of(me, width)],
        send.at[step],
        recv.at[step],
        "seq",
        peer,
    )
    copy.start()
    return copy


def join_rows(src, dst, send, recv, me, size):
    rows = dst.shape[0]
    width = src.shape[1]
    copies = [join_block(src, dst, send, recv, me, size, step) for step in range(1, size)]
    dst[:, rows_of(me, width)] = src[rows_of(me, rows), :]
    return copies


def swap_slots(src, dst, send, recv, me, size):
    cap = src.shape[0] // size
    copies = []
    for step in range(1, size):
        peer = lax.rem(me + step, size)
        copy = remote(
            src.at[rows_of(peer, cap), :],
            dst.at[rows_of(me, cap), :],
            send.at[step],
            recv.at[step],
            "expert",
            peer,
        )
        copy.start()
        copies.append(copy)
    dst[rows_of(me, cap), :] = src[rows_of(me, cap), :]
    return copies


def arrive(copies):
    for copy in copies:
        copy.wait_recv()


def softmax_rows(query, key):
    scores = dot_nt(query, key) * (1.0 / math.sqrt(DH))
    exponent = jnp.exp(scores - jnp.max(scores, axis=-1, keepdims=True))
    return exponent / jnp.sum(exponent, axis=-1, keepdims=True)


def as_column(row):
    size = row.shape[1]
    same = lax.broadcasted_iota(jnp.int32, (size, size), 0) == lax.broadcasted_iota(
        jnp.int32, (size, size), 1
    )
    return jnp.sum(jnp.where(same, row, 0.0), axis=1, keepdims=True)


def layer_kernel(
    experts, cap, chunk,
    q_hbm, k_hbm, v_hbm, routes_ref, gates_ref, up_hbm, down_hbm, cot_ref,
    layer_ref, gq_ref, gk_ref, gv_ref, gup_ref, gdown_ref,
    qh, kh, vh, heads, att, probs, datt, dheads, gqh, gkh, gvh,
    place, sent_grad, grad_in, sent_rows, rows_in, out_rows, dnorm_rows, ret_out, ret_dnorm,
    up, down, dact, act, dpre, rows_t, grad_t,
    gw_own, gw_other, gw_recv, a1_recv, b1_recv, a2_sent, a2_recv, b2_sent, b2_recv,
    seq_send, seq_recv, exp_send, exp_recv, dp_send, dp_recv, red_send, red_recv, local_sem,
):
    n_seq = lax.axis_size("seq")
    n_exp = lax.axis_size("expert")
    me_seq = lax.axis_index("seq")
    me_exp = lax.axis_index("expert")
    me_dp = lax.axis_index("dp")
    rows = cot_ref.shape[0]
    slots = experts * cap
    model, hidden = up.shape
    width = heads.shape[1]
    n_heads = width // DH
    sent = []

    load_down = pltpu.make_async_copy(down_hbm, down, local_sem.at[0])
    load_up = pltpu.make_async_copy(up_hbm, up, local_sem.at[1])
    greet(("seq", "expert", "dp"))

    seq_copies = []
    own_copies = []
    for number, (src, dst) in enumerate(((q_hbm, qh), (k_hbm, kh), (v_hbm, vh))):
        copies, own = split_cols(
            src, dst, seq_send.at[number], seq_recv.at[number], me_seq, n_seq,
            local_sem.at[2 + number],
        )
        seq_copies += copies
        own_copies.append(own)
    load_down.start()
    load_up.start()

    expert_ids = lax.broadcasted_iota(jnp.int32, (experts, rows), 0)
    hits = [
        jnp.where(routes_ref[j : j + 1, :] == expert_ids, 1.0, 0.0).astype(F32)
        for j in range(TOP)
    ]
    earlier = lax.broadcasted_iota(jnp.int32, (rows, rows), 0) < lax.broadcasted_iota(
        jnp.int32, (rows, rows), 1
    )
    rank = dot_nn(
        (hits[0] + hits[1]).astype(BF16), jnp.where(earlier, 1.0, 0.0).astype(BF16)
    )
    base = rank + (expert_ids * cap).astype(F32)
    slot_ids = lax.broadcasted_iota(jnp.int32, (slots, rows), 0).astype(F32)
    cot = cot_ref[...].astype(F32)
    gates = [as_column(gates_ref[j : j + 1, :]) for j in range(TOP)]
    packed = None
    for j in range(TOP):
        slot = jnp.sum(hits[j] * base, axis=0, keepdims=True)
        place[j] = jnp.where(slot_ids == slot, 1.0, 0.0).astype(BF16)
        part = dot_nn(place[j], (gates[j] * cot).astype(BF16))
        packed = part if packed is None else packed + part
    sent_grad[...] = packed.astype(BF16)
    grad_copies = swap_slots(sent_grad, grad_in, exp_send.at[0], exp_recv.at[0], me_exp, n_exp)
    sent += seq_copies + grad_copies

    for own in own_copies:
        own.wait()
    arrive(seq_copies)
    back = []
    for step in [*range(1, n_seq), 0]:
        block = rows_of(lax.rem(me_seq + step, n_seq), rows)
        for head in range(n_heads):
            cols = slice(head * DH, (head + 1) * DH)
            prob = softmax_rows(qh[block, cols], kh[:, cols])
            probs[head, block, :] = prob
            heads[block, cols] = dot_nn(prob.astype(BF16), vh[:, cols]).astype(BF16)
        if step > 0:
            back.append(
                join_block(heads, att, seq_send.at[3], seq_recv.at[3], me_seq, n_seq, step)
            )
        else:
            att[:, rows_of(me_seq, width)] = heads[block, :]
    arrive(back)
    sent += back

    att_f = att[...].astype(F32)
    inverse = lax.rsqrt(jnp.mean(att_f * att_f, axis=-1, keepdims=True) + EPSILON)
    placer = place[0] + place[1]
    sent_rows[...] = dot_nn(placer, (att_f * inverse).astype(BF16)).astype(BF16)
    row_copies = swap_slots(sent_rows, rows_in, exp_send.at[1], exp_recv.at[1], me_exp, n_exp)
    sent += row_copies
    arrive(grad_copies)
    load_down.wait()
    load_up.wait()

    @pl.loop(0, hidden // chunk)
    def _(c):
        cols = rows_of(c, chunk)
        dact[:, cols] = dot_nt(grad_in[...], down[cols, :])

    grad_t[...] = grad_in[...].T
    arrive(row_copies)

    @pl.loop(0, hidden // chunk)
    def _(c):
        cols = rows_of(c, chunk)
        value, slope = gelu_pair(dot_nn(rows_in[...], up[:, cols]))
        act[:, cols] = value.astype(BF16)
        dpre[:, cols] = (dact[:, cols] * slope).astype(BF16)

    @pl.loop(0, model // 256)
    def _(c):
        cols = rows_of(c, 256)
        dnorm_rows[:, cols] = dot_nt(dpre[...], up[cols, :]).astype(BF16)

    dnorm_copies = swap_slots(
        dnorm_rows, ret_dnorm, exp_send.at[2], exp_recv.at[2], me_exp, n_exp
    )
    sent += dnorm_copies

    rows_t[...] = rows_in[...].T
    half = model // 2
    part_rows = half // 2
    dp_copies = []

    def weight_grads(dst, start, base_row):
        @pl.loop(0, hidden // chunk)
        def _(c):
            cols = rows_of(c, chunk)
            later = pl.ds(pl.multiple_of(hidden + c * chunk, chunk), chunk)
            lines = pl.ds(pl.multiple_of(base_row + start, part_rows), part_rows)
            here = slice(start, start + part_rows)
            dst[here, cols] = dot_nn(rows_t[lines, :], dpre[:, cols]).astype(BF16)
            dst[here, later] = dot_nn(grad_t[lines, :], act[:, cols]).astype(BF16)

    for number in range(2):
        start = number * part_rows
        weight_grads(gw_other, start, (1 - me_dp) * half)
        copy = remote(
            gw_other.at[start : start + part_rows, :],
            gw_recv.at[start : start + part_rows, :],
            dp_send.at[number],
            dp_recv.at[number],
            "dp",
            1 - me_dp,
        )
        copy.start()
        dp_copies.append(copy)
    sent += dp_copies
    for number in range(2):
        weight_grads(gw_own, number * part_rows, me_dp * half)

    low = lax.rem(me_seq, 2)
    high = me_seq // 2
    peer_low = 2 * high + 1 - low
    peer_high = 2 * (1 - high) + low
    piece = half // n_seq
    first = slice(0, hidden)
    second = slice(hidden, 2 * hidden)

    def reduce_send(src, dst, number, peer):
        copy = remote(src, dst, red_send.at[number], red_recv.at[number], "seq", peer)
        copy.start()
        sent.append(copy)
        return copy

    a1, b1 = [], []
    for number in range(2):
        dp_copies[number].wait_recv()

        @pl.loop(0, 2 * hidden // chunk)
        def _(c):
            cols = rows_of(c, chunk)
            here = slice(number * part_rows, (number + 1) * part_rows)
            gw_own[here, cols] = (
                gw_own[here, cols].astype(F32) + gw_recv[here, cols].astype(F32)
            ).astype(BF16)

        a1.append(
            reduce_send(
                gw_own.at[rows_of(2 * number + 1 - low, piece), first],
                a1_recv.at[number], number, peer_low,
            )
        )
    for number in range(2):
        b1.append(
            reduce_send(
                gw_own.at[rows_of(2 * (1 - high) + number, piece), second],
                b1_recv.at[number], 2 + number, peer_high,
            )
        )

    @pl.loop(0, model // 256)
    def _(c):
        cols = rows_of(c, 256)
        out_rows[:, cols] = dot_nn(act[...], down[:, cols]).astype(BF16)

    out_copies = swap_slots(out_rows, ret_out, exp_send.at[3], exp_recv.at[3], me_exp, n_exp)
    sent += out_copies

    arrive(dnorm_copies)
    dunit = dot_tn(place[0] + place[1], ret_dnorm[...])
    att_f = att[...].astype(F32)
    inverse = lax.rsqrt(jnp.mean(att_f * att_f, axis=-1, keepdims=True) + EPSILON)
    unit = att_f * inverse
    datt[...] = (
        cot_ref[...].astype(F32)
        + inverse * (dunit - unit * jnp.mean(dunit * unit, axis=-1, keepdims=True))
    ).astype(BF16)
    datt_copies, own = split_cols(
        datt, dheads, seq_send.at[4], seq_recv.at[4], me_seq, n_seq, local_sem.at[5]
    )
    sent += datt_copies
    own.wait()
    arrive(datt_copies)

    scaling = 1.0 / math.sqrt(DH)
    for head in range(n_heads):
        cols = slice(head * DH, (head + 1) * DH)
        prob = probs[head]
        dhead = dheads[:, cols]
        gvh[:, cols] = dot_tn(prob.astype(BF16), dhead).astype(BF16)
        dprobs = dot_nt(dhead, vh[:, cols])
        delta = jnp.sum(prob * dprobs, axis=-1, keepdims=True)
        dscores = (prob * (dprobs - delta) * scaling).astype(BF16)
        gkh[:, cols] = dot_tn(dscores, qh[:, cols]).astype(BF16)
        gqh[:, cols] = dot_nn(dscores, kh[:, cols]).astype(BF16)
    last = []
    for number, (src, dst) in enumerate(((gvh, gv_ref), (gkh, gk_ref), (gqh, gq_ref)), 5):
        last += join_rows(src, dst, seq_send.at[number], seq_recv.at[number], me_seq, n_seq)
    sent += last

    arrive(a1)
    a2_sent[...] = (
        gw_own[rows_of(2 * (1 - high) + low, piece), first].astype(F32)
        + a1_recv[1 - high].astype(F32)
    ).astype(BF16)
    a2 = reduce_send(a2_sent, a2_recv, 4, peer_high)
    arrive(b1)
    b2_sent[...] = (
        gw_own[rows_of(2 * high + 1 - low, piece), second].astype(F32)
        + b1_recv[1 - low].astype(F32)
    ).astype(BF16)
    b2 = reduce_send(b2_sent, b2_recv, 5, peer_low)

    arrive(out_copies)
    mix = None
    for j in range(TOP):
        part = as_column(gates_ref[j : j + 1, :]) * dot_tn(place[j], ret_out[...])
        mix = part if mix is None else mix + part
    layer_ref[...] = (att[...].astype(F32) + mix).astype(BF16)

    mine = rows_of(me_seq, piece)
    a2.wait_recv()
    gup_ref[...] = (
        gw_own[mine, first].astype(F32) + a1_recv[high].astype(F32) + a2_recv[...].astype(F32)
    )
    b2.wait_recv()
    gdown_ref[...] = (
        gw_own[mine, second].astype(F32) + b1_recv[low].astype(F32) + b2_recv[...].astype(F32)
    ).T
    arrive(last)
    for copy in sent:
        copy.wait_send()


def shards(
    query_input, key_input, value_input, routes, gate_values, up_weight, down_weight, cotangent
):
    rows, model = query_input.shape[1:]
    n_seq = lax.axis_size("seq")
    n_exp = lax.axis_size("expert")
    hidden = up_weight.shape[2]
    experts = up_weight.shape[0] * n_exp
    cap = rows * TOP * 3 // (2 * experts)
    cap = -(-cap // 16) * 16
    slots = experts * cap
    width = model // n_seq
    tokens = rows * n_seq
    half = model // 2
    piece = half // n_seq
    vmem = pl.BlockSpec(memory_space=pltpu.VMEM)
    hbm = pl.BlockSpec(memory_space=pl.ANY)
    dma = pltpu.SemaphoreType.DMA

    def shape(*dims, dtype=BF16):
        return jax.ShapeDtypeStruct(dims, dtype)

    def buf(*dims, dtype=BF16):
        return pltpu.VMEM(dims, dtype)

    head_block = buf(tokens, width)
    slot_block = buf(slots, model)
    layer, grad_q, grad_k, grad_v, grad_up, grad_down = pl.pallas_call(
        functools.partial(layer_kernel, experts, cap, 512),
        name="layer",
        out_shape=[shape(rows, model)] * 4
        + [shape(piece, hidden, dtype=F32), shape(hidden, piece, dtype=F32)],
        in_specs=[hbm] * 3 + [vmem] * 2 + [hbm] * 2 + [vmem],
        out_specs=[vmem] * 6,
        scratch_shapes=[
            head_block, head_block, head_block, head_block,
            buf(rows, model),
            buf(width // DH, tokens, tokens, dtype=F32),
            buf(rows, model),
            head_block, head_block, head_block, head_block,
            buf(TOP, slots, rows),
            slot_block, slot_block, slot_block, slot_block,
            slot_block, slot_block, slot_block, slot_block,
            buf(model, hidden),
            buf(hidden, model),
            buf(slots, hidden, dtype=F32),
            buf(slots, hidden),
            buf(slots, hidden),
            buf(model, slots),
            buf(model, slots),
            buf(half, 2 * hidden),
            buf(half, 2 * hidden),
            buf(half, 2 * hidden),
            buf(2, piece, hidden),
            buf(2, piece, hidden),
            buf(piece, hidden), buf(piece, hidden), buf(piece, hidden), buf(piece, hidden),
            dma((8, n_seq)),
            dma((8, n_seq)),
            dma((4, n_exp)),
            dma((4, n_exp)),
            dma((2,)),
            dma((2,)),
            dma((6,)),
            dma((6,)),
            dma((6,)),
        ],
        compiler_params=pltpu.CompilerParams(
            collective_id=0, has_side_effects=True, vmem_limit_bytes=VMEM_LIMIT
        ),
        cost_estimate=pl.CostEstimate(
            flops=12 * slots * model * hidden, bytes_accessed=16 * model * hidden,
            transcendentals=0,
        ),
    )(
        query_input[0], key_input[0], value_input[0], routes[0].T, gate_values[0].T,
        up_weight[0], down_weight[0], cotangent[0],
    )
    return (
        layer[None], grad_q[None], grad_k[None], grad_v[None], grad_up[None], grad_down[None]
    )


def solution(mesh):
    tokens = P(("dp", "expert"), "seq", None)
    weights = P("expert", None, None)
    in_specs = (tokens,) * 5 + (weights, weights, tokens)
    out_specs = (tokens,) * 4 + (P("expert", ("dp", "seq"), None), P("expert", None, ("dp", "seq")))
    return jax.shard_map(shards, mesh=mesh, in_specs=in_specs, out_specs=out_specs, check_vma=False)
```

time: 176 us -> 120 us (0.68)
  waiting for transfers between devices: 37.6 us -> 0 us
  between operations: 14.1 us -> 0.65 us
  local copies, waits for them, and re-layouts: 12.6 us -> 10 us
    reduce_scatter x2 -> x0, waiting for transfers between devices: 37.6 us -> none  [the longest x1 20.2 us: shards(): summed = lax.psum_scatter(halves, 'seq', scatter_dimension=0, tiled=True)]
    unnamed x23 -> x8, local copies, waits for them, and re-layouts: 11.4 us -> 10 us
    pallas_call x3 -> x1, Pallas kernels: 108 us -> 109 us  [shards(): pl.pallas_call(functools.partial(layer_kernel, experts, cap, 512), name='...]
  transfers between devices with their start and end apart: 2 -> 0, of which waited for: 2 -> 0; matrix products, arithmetic and copies ran while one was open for 0% -> 0% of each run, Pallas kernels for 27% -> 0%
where the time goes in v2:
time: 120 us; the launch traced here: 119 us
  Pallas kernels  109 us (91%)
  local copies, waits for them, and re-layouts  10 us (8%)
    pallas_call x1, Pallas kernels, shards(): pl.pallas_call(functools.partial(layer_kernel, experts, cap, 512), name='...  109 us
    unnamed x8, local copies, waits for them, and re-layouts  10 us

profile of v2, /device:TPU:24, one launch (start us, length us, event | category | flops | bytes accessed | tf_op | source)
XLA Modules:
  0.0 119.3 jit_solution(7100805864847309912)
XLA Ops:
  0.6 108.6 %layer.1 = (bf16[128,1024]{1,0:T(8,128)(2,1)}, bf16[128,1024]{1,0:T(8,128)(2,1)}, bf16[128,1024]{1,0:T(8,128)(2,1)}, bf16[128,1024]{1,0:T(8,128)(2,1)}, f32[128,2048]{1,0:T(8,128)}, /*index=5*/f32[2048,128]{1,0:T(8,128)}) custom-call(bf16[128,1024]{1,0:T(8,128)(2,1)} %bitcast.26, bf16[128,1024]{1,0:T(8,128)(2,1)} %bitcast.27, bf16[128,1024]{1,0:T(8,128)(2,1)} %bitcast.28, ...), custom_call_target="tpu_custom_call" | custom-call | flops 9663676416 | bytes 33554432 | tf_op jit(solution)/shard_map/layer/pallas_call | solution.py:446
  109.3 0.0 copy-start
  109.3 1.8 %copy.20 = bf16[1,128,1024]{2,1,0:T(8,128)(2,1)} copy(bf16[1,128,1024]{2,1,0:T(8,128)(2,1)} %bitcast.23) | data formatting | bytes 524288
  111.1 1.7 %copy.21 = bf16[1,128,1024]{2,1,0:T(8,128)(2,1)} copy(bf16[1,128,1024]{2,1,0:T(8,128)(2,1)} %bitcast.22) | data formatting | bytes 524288
  112.7 1.7 %copy.22 = bf16[1,128,1024]{2,1,0:T(8,128)(2,1)} copy(bf16[1,128,1024]{2,1,0:T(8,128)(2,1)} %bitcast.21) | data formatting | bytes 524288
  114.4 1.7 %copy.23 = bf16[1,128,1024]{2,1,0:T(8,128)(2,1)} copy(bf16[1,128,1024]{2,1,0:T(8,128)(2,1)} %bitcast.20) | data formatting | bytes 524288
  116.1 2.3 %copy.24 = f32[1,128,2048]{2,1,0:T(8,128)} copy(f32[1,128,2048]{2,1,0:T(8,128)} %bitcast.19) | data formatting | bytes 2097152
  118.4 0.0 copy-done
  118.4 1.0 copy.25
Async XLA Ops:
  109.3 9.1 %copy-start = (f32[2048,128]{1,0:T(8,128)S(1)}, f32[2048,128]{1,0:T(8,128)}, u32[]{:S(2)}) copy-start(f32[2048,128]{1,0:T(8,128)} %get-tuple-element.17) | copy-start | bytes 3145732

commit v3 on v2

--- a/solution.py
+++ b/solution.py
@@ -155,7 +155,8 @@
 def layer_kernel(
     experts, cap, chunk,
     q_hbm, k_hbm, v_hbm, routes_ref, gates_ref, up_hbm, down_hbm, cot_ref,
-    layer_ref, gq_ref, gk_ref, gv_ref, gup_ref, gdown_ref,
+    layer_out, gq_out, gk_out, gv_out, gup_out, gdown_out,
+    layer, gq, gk, gv, gup, gdown,
     qh, kh, vh, heads, att, probs, datt, dheads, gqh, gkh, gvh,
     place, sent_grad, grad_in, sent_rows, rows_in, out_rows, dnorm_rows, ret_out, ret_dnorm,
     up, down, dact, act, dpre, rows_t, grad_t,
@@ -260,55 +261,49 @@
         act[:, cols] = value.astype(BF16)
         dpre[:, cols] = (dact[:, cols] * slope).astype(BF16)
 
-    @pl.loop(0, model // 256)
-    def _(c):
-        cols = rows_of(c, 256)
-        dnorm_rows[:, cols] = dot_nt(dpre[...], up[cols, :]).astype(BF16)
-
-    dnorm_copies = swap_slots(
-        dnorm_rows, ret_dnorm, exp_send.at[2], exp_recv.at[2], me_exp, n_exp
-    )
-    sent += dnorm_copies
-
     rows_t[...] = rows_in[...].T
     half = model // 2
-    part_rows = half // 2
-    dp_copies = []
-
-    def weight_grads(dst, start, base_row):
-        @pl.loop(0, hidden // chunk)
-        def _(c):
-            cols = rows_of(c, chunk)
-            later = pl.ds(pl.multiple_of(hidden + c * chunk, chunk), chunk)
-            lines = pl.ds(pl.multiple_of(base_row + start, part_rows), part_rows)
-            here = slice(start, start + part_rows)
-            dst[here, cols] = dot_nn(rows_t[lines, :], dpre[:, cols]).astype(BF16)
-            dst[here, later] = dot_nn(grad_t[lines, :], act[:, cols]).astype(BF16)
-
-    for number in range(2):
-        start = number * part_rows
-        weight_grads(gw_other, start, (1 - me_dp) * half)
-        copy = remote(
-            gw_other.at[start : start + part_rows, :],
-            gw_recv.at[start : start + part_rows, :],
-            dp_send.at[number],
-            dp_recv.at[number],
-            "dp",
-            1 - me_dp,
-        )
-        copy.start()
-        dp_copies.append(copy)
-    sent += dp_copies
-    for number in range(2):
-        weight_grads(gw_own, number * part_rows, me_dp * half)
-
+    piece = half // n_seq
+    pair = 2 * piece
     low = lax.rem(me_seq, 2)
     high = me_seq // 2
     peer_low = 2 * high + 1 - low
     peer_high = 2 * (1 - high) + low
-    piece = half // n_seq
-    first = slice(0, hidden)
-    second = slice(hidden, 2 * hidden)
+
+    def grads_first(dst, core, bit):
+        left = jnp.concatenate(
+            [rows_t[rows_of(core * n_seq + 2 * n + bit, piece), :] for n in range(2)], axis=0
+        )
+
+        @pl.loop(0, hidden // chunk)
+        def _(c):
+            cols = rows_of(c, chunk)
+            dst[:, cols] = dot_nn(left, dpre[:, cols]).astype(BF16)
+
+    def grads_second(dst, core, bit):
+        left = grad_t[rows_of(core * (n_seq // 2) + bit, pair), :]
+
+        @pl.loop(0, hidden // chunk)
+        def _(c):
+            cols = rows_of(c, chunk)
+            dst[:, cols] = dot_nn(left, act[:, cols]).astype(BF16)
+
+    def core_send(number):
+        copy = remote(
+            gw_other.at[number], gw_recv.at[number], dp_send.at[number], dp_recv.at[number],
+            "dp", 1 - me_dp,
+        )
+        copy.start()
+        sent.append(copy)
+        return copy
+
+    def add_core(number):
+        @pl.loop(0, hidden // chunk)
+        def _(c):
+            cols = rows_of(c, chunk)
+            gw_own[number, :, cols] = (
+                gw_own[number, :, cols].astype(F32) + gw_recv[number, :, cols].astype(F32)
+            ).astype(BF16)
 
     def reduce_send(src, dst, number, peer):
         copy = remote(src, dst, red_send.at[number], red_recv.at[number], "seq", peer)
@@ -316,41 +311,60 @@
         sent.append(copy)
         return copy
 
-    a1, b1 = [], []
-    for number in range(2):
-        dp_copies[number].wait_recv()
-
-        @pl.loop(0, 2 * hidden // chunk)
-        def _(c):
-            cols = rows_of(c, chunk)
-            here = slice(number * part_rows, (number + 1) * part_rows)
-            gw_own[here, cols] = (
-                gw_own[here, cols].astype(F32) + gw_recv[here, cols].astype(F32)
-            ).astype(BF16)
-
+    grads_first(gw_other.at[0], 1 - me_dp, 1 - low)
+    core_first = core_send(0)
+    grads_second(gw_other.at[1], 1 - me_dp, 1 - high)
+    core_second = core_send(1)
+    grads_first(gw_own.at[0], me_dp, 1 - low)
+    grads_second(gw_own.at[1], me_dp, 1 - high)
+
+    @pl.loop(0, model // 256)
+    def _(c):
+        cols = rows_of(c, 256)
+        dnorm_rows[:, cols] = dot_nt(dpre[...], up[cols, :]).astype(BF16)
+
+    dnorm_copies = swap_slots(
+        dnorm_rows, ret_dnorm, exp_send.at[2], exp_recv.at[2], me_exp, n_exp
+    )
+    sent += dnorm_copies
+
+    core_first.wait_recv()
+    add_core(0)
+    a1 = []
+    for number, which in enumerate((1 - high, high)):
         a1.append(
-            reduce_send(
-                gw_own.at[rows_of(2 * number + 1 - low, piece), first],
-                a1_recv.at[number], number, peer_low,
-            )
-        )
-    for number in range(2):
+            reduce_send(gw_own.at[0, rows_of(which, piece), :], a1_recv.at[which], number, peer_low)
+        )
+    core_second.wait_recv()
+    add_core(1)
+    b1 = []
+    for number, which in enumerate((1 - low, low), 2):
         b1.append(
             reduce_send(
-                gw_own.at[rows_of(2 * (1 - high) + number, piece), second],
-                b1_recv.at[number], 2 + number, peer_high,
+                gw_own.at[1, rows_of(which, piece), :], b1_recv.at[which], number, peer_high
             )
         )
+
+    grads_first(gw_other.at[2], 1 - me_dp, low)
+    core_third = core_send(2)
+    grads_second(gw_other.at[3], 1 - me_dp, high)
+    core_fourth = core_send(3)
+    grads_first(gw_own.at[2], me_dp, low)
+    grads_second(gw_own.at[3], me_dp, high)
 
     @pl.loop(0, model // 256)
     def _(c):
         cols = rows_of(c, 256)
         out_rows[:, cols] = dot_nn(act[...], down[:, cols]).astype(BF16)
 
+    core_third.wait_recv()
+    add_core(2)
+    core_fourth.wait_recv()
+    add_core(3)
+
+    arrive(dnorm_copies)
     out_copies = swap_slots(out_rows, ret_out, exp_send.at[3], exp_recv.at[3], me_exp, n_exp)
     sent += out_copies
-
-    arrive(dnorm_copies)
     dunit = dot_tn(place[0] + place[1], ret_dnorm[...])
     att_f = att[...].astype(F32)
     inverse = lax.rsqrt(jnp.mean(att_f * att_f, axis=-1, keepdims=True) + EPSILON)
@@ -378,20 +392,18 @@
         gkh[:, cols] = dot_tn(dscores, qh[:, cols]).astype(BF16)
         gqh[:, cols] = dot_nn(dscores, kh[:, cols]).astype(BF16)
     last = []
-    for number, (src, dst) in enumerate(((gvh, gv_ref), (gkh, gk_ref), (gqh, gq_ref)), 5):
+    for number, (src, dst) in enumerate(((gvh, gv), (gkh, gk), (gqh, gq)), 5):
         last += join_rows(src, dst, seq_send.at[number], seq_recv.at[number], me_seq, n_seq)
     sent += last
 
-    arrive(a1)
+    a1[0].wait_recv()
     a2_sent[...] = (
-        gw_own[rows_of(2 * (1 - high) + low, piece), first].astype(F32)
-        + a1_recv[1 - high].astype(F32)
+        gw_own[2, rows_of(1 - high, piece), :].astype(F32) + a1_recv[1 - high].astype(F32)
     ).astype(BF16)
     a2 = reduce_send(a2_sent, a2_recv, 4, peer_high)
-    arrive(b1)
+    b1[0].wait_recv()
     b2_sent[...] = (
-        gw_own[rows_of(2 * high + 1 - low, piece), second].astype(F32)
-        + b1_recv[1 - low].astype(F32)
+        gw_own[3, rows_of(1 - low, piece), :].astype(F32) + b1_recv[1 - low].astype(F32)
     ).astype(BF16)
     b2 = reduce_send(b2_sent, b2_recv, 5, peer_low)
 
@@ -400,20 +412,50 @@
     for j in range(TOP):
         part = as_column(gates_ref[j : j + 1, :]) * dot_tn(place[j], ret_out[...])
         mix = part if mix is None else mix + part
-    layer_ref[...] = (att[...].astype(F32) + mix).astype(BF16)
-
-    mine = rows_of(me_seq, piece)
+    layer[...] = (att[...].astype(F32) + mix).astype(BF16)
+    stores = []
+
+    def store(src, dst):
+        copy = pltpu.make_async_copy(src, dst, local_sem.at[6 + len(stores)])
+        copy.start()
+        stores.append(copy)
+
+    store(layer, layer_out)
+    a1[1].wait_recv()
+    b1[1].wait_recv()
+    for number, (src, dst) in enumerate(((gv, gv_out), (gk, gk_out), (gq, gq_out))):
+        arrive(last[number * (n_seq - 1) : (number + 1) * (n_seq - 1)])
+        store(src, dst)
     a2.wait_recv()
-    gup_ref[...] = (
-        gw_own[mine, first].astype(F32) + a1_recv[high].astype(F32) + a2_recv[...].astype(F32)
-    )
+    gup[...] = (
+        gw_own[2, rows_of(high, piece), :].astype(F32)
+        + a1_recv[high].astype(F32)
+        + a2_recv[...].astype(F32)
+    )
+    store(gup, gup_out)
     b2.wait_recv()
-    gdown_ref[...] = (
-        gw_own[mine, second].astype(F32) + b1_recv[low].astype(F32) + b2_recv[...].astype(F32)
+    gdown[...] = (
+        gw_own[3, rows_of(low, piece), :].astype(F32)
+        + b1_recv[low].astype(F32)
+        + b2_recv[...].astype(F32)
     ).T
-    arrive(last)
+    store(gdown, gdown_out)
     for copy in sent:
         copy.wait_send()
+    for copy in stores:
+        copy.wait()
+
+
+def copy_kernel(*refs):
+    count = (len(refs) - 1) // 2
+    sems = refs[-1]
+    copies = [
+        pltpu.make_async_copy(refs[n], refs[count + n], sems.at[n]) for n in range(count)
+    ]
+    for copy in copies:
+        copy.start()
+    for copy in copies:
+        copy.wait()
 
 
 def shards(
@@ -443,14 +485,21 @@
 
     head_block = buf(tokens, width)
     slot_block = buf(slots, model)
-    layer, grad_q, grad_k, grad_v, grad_up, grad_down = pl.pallas_call(
+    row_block = buf(rows, model)
+    out_shapes = [shape(rows, model)] * 4 + [
+        shape(piece, hidden, dtype=F32),
+        shape(hidden, piece, dtype=F32),
+    ]
+    results = pl.pallas_call(
         functools.partial(layer_kernel, experts, cap, 512),
         name="layer",
-        out_shape=[shape(rows, model)] * 4
-        + [shape(piece, hidden, dtype=F32), shape(hidden, piece, dtype=F32)],
+        out_shape=out_shapes,
         in_specs=[hbm] * 3 + [vmem] * 2 + [hbm] * 2 + [vmem],
-        out_specs=[vmem] * 6,
+        out_specs=[hbm] * 6,
         scratch_shapes=[
+            row_block, row_block, row_block, row_block,
+            buf(piece, hidden, dtype=F32),
+            buf(hidden, piece, dtype=F32),
             head_block, head_block, head_block, head_block,
             buf(rows, model),
             buf(width // DH, tokens, tokens, dtype=F32),
@@ -466,9 +515,9 @@
             buf(slots, hidden),
             buf(model, slots),
             buf(model, slots),
-            buf(half, 2 * hidden),
-            buf(half, 2 * hidden),
-            buf(half, 2 * hidden),
+            buf(4, 2 * piece, hidden),
+            buf(4, 2 * piece, hidden),
+            buf(4, 2 * piece, hidden),
             buf(2, piece, hidden),
             buf(2, piece, hidden),
             buf(piece, hidden), buf(piece, hidden), buf(piece, hidden), buf(piece, hidden),
@@ -476,11 +525,11 @@
             dma((8, n_seq)),
             dma((4, n_exp)),
             dma((4, n_exp)),
-            dma((2,)),
-            dma((2,)),
+            dma((4,)),
+            dma((4,)),
             dma((6,)),
             dma((6,)),
-            dma((6,)),
+            dma((12,)),
         ],
         compiler_params=pltpu.CompilerParams(
             collective_id=0, has_side_effects=True, vmem_limit_bytes=VMEM_LIMIT
@@ -493,9 +542,16 @@
         query_input[0], key_input[0], value_input[0], routes[0].T, gate_values[0].T,
         up_weight[0], down_weight[0], cotangent[0],
     )
-    return (
-        layer[None], grad_q[None], grad_k[None], grad_v[None], grad_up[None], grad_down[None]
-    )
+    results = pl.pallas_call(
+        copy_kernel,
+        name="outputs",
+        out_shape=out_shapes,
+        in_specs=[hbm] * 6,
+        out_specs=[hbm] * 6,
+        scratch_shapes=[dma((6,))],
+        compiler_params=pltpu.CompilerParams(vmem_limit_bytes=VMEM_LIMIT),
+    )(*results)
+    return tuple(result[None] for result in results)
 
 
 def solution(mesh):

time: 120 us -> 203 us (1.69)
  Pallas kernels: 109 us -> 202 us
  local copies, waits for them, and re-layouts: 10 us -> 0 us
    pallas_call x0 -> x1, Pallas kernels: none -> 96.5 us  [shards(): pl.pallas_call(copy_kernel, name='outputs', out_shape=out_shapes, in_spec...]
    unnamed x8 -> x0, local copies, waits for them, and re-layouts: 10 us -> none
    pallas_call x1, Pallas kernels: 109 us -> 106 us  [shards(): pl.pallas_call(functools.partial(layer_kernel, experts, cap, 512), name='...]
where the time goes in v3:
time: 203 us
  Pallas kernels  202 us (100%)
    pallas_call x1, Pallas kernels, shards(): pl.pallas_call(functools.partial(layer_kernel, experts, cap, 512), name='...  106 us
    pallas_call x1, Pallas kernels, shards(): pl.pallas_call(copy_kernel, name='outputs', out_shape=out_shapes, in_spec...  96.5 us

profile of v3, /device:TPU:24, one launch (start us, length us, event | category | flops | bytes accessed | tf_op | source)
XLA Modules:
  0.0 203.0 jit_solution(6461418377519482063)
XLA Ops:
  0.6 105.9 %layer.1 = (bf16[128,1024]{1,0:T(8,128)(2,1)}, bf16[128,1024]{1,0:T(8,128)(2,1)}, bf16[128,1024]{1,0:T(8,128)(2,1)}, bf16[128,1024]{1,0:T(8,128)(2,1)}, f32[128,2048]{1,0:T(8,128)}, /*index=5*/f32[2048,128]{1,0:T(8,128)}) custom-call(bf16[128,1024]{1,0:T(8,128)(2,1)} %bitcast.22, bf16[128,1024]{1,0:T(8,128)(2,1)} %bitcast.23, bf16[128,1024]{1,0:T(8,128)(2,1)} %bitcast.24, ...), custom_call_target="tpu_custom_call" | custom-call | flops 9663676416 | bytes 33554432 | tf_op jit(solution)/shard_map/layer/pallas_call | solution.py:493
  106.6 96.5 %outputs.1 = (bf16[128,1024]{1,0:T(8,128)(2,1)}, bf16[128,1024]{1,0:T(8,128)(2,1)}, bf16[128,1024]{1,0:T(8,128)(2,1)}, bf16[128,1024]{1,0:T(8,128)(2,1)}, f32[128,2048]{1,0:T(8,128)}, /*index=5*/f32[2048,128]{1,0:T(8,128)}) custom-call(bf16[128,1024]{1,0:T(8,128)(2,1)} %get-tuple-element.18.refs_0_, bf16[128,1024]{1,0:T(8,128)(2,1)} %get-tuple-element.19.refs_1_, ...), custom_call_target="tpu_custom_call" | custom-call | tf_op jit(solution)/shard_map/outputs/pallas_call | solution.py:545

commit v4 on v3

--- a/solution.py
+++ b/solution.py
@@ -447,15 +447,21 @@
 
 
 def copy_kernel(*refs):
-    count = (len(refs) - 1) // 2
-    sems = refs[-1]
-    copies = [
-        pltpu.make_async_copy(refs[n], refs[count + n], sems.at[n]) for n in range(count)
+    count = (len(refs) - 1) // 3
+    sources, targets, held, sems = refs[:count], refs[count : 2 * count], refs[2 * count : -1], refs[-1]
+    loads = [
+        pltpu.make_async_copy(sources[n], held[n], sems.at[n]) for n in range(count)
     ]
-    for copy in copies:
-        copy.start()
-    for copy in copies:
-        copy.wait()
+    saves = [
+        pltpu.make_async_copy(held[n], targets[n], sems.at[count + n]) for n in range(count)
+    ]
+    for load in loads:
+        load.start()
+    for load, save in zip(loads, saves):
+        load.wait()
+        save.start()
+    for save in saves:
+        save.wait()
 
 
 def shards(
@@ -548,7 +554,7 @@
         out_shape=out_shapes,
         in_specs=[hbm] * 6,
         out_specs=[hbm] * 6,
-        scratch_shapes=[dma((6,))],
+        scratch_shapes=[pltpu.VMEM(out.shape, out.dtype) for out in out_shapes] + [dma((12,))],
         compiler_params=pltpu.CompilerParams(vmem_limit_bytes=VMEM_LIMIT),
     )(*results)
     return tuple(result[None] for result in results)

time: 203 us -> 110 us (0.54)
  Pallas kernels: 202 us -> 109 us
    pallas_call x1, Pallas kernels: 96.5 us -> 2.97 us  [shards(): pl.pallas_call(copy_kernel, name='outputs', out_shape=out_shapes, in_spec...]
where the time goes in v4:
time: 110 us
  Pallas kernels  109 us (99%)
    pallas_call x1, Pallas kernels, shards(): pl.pallas_call(functools.partial(layer_kernel, experts, cap, 512), name='...  106 us
    pallas_call x1, Pallas kernels, shards(): pl.pallas_call(copy_kernel, name='outputs', out_shape=out_shapes, in_spec...  2.97 us

profile of v4, /device:TPU:24, one launch (start us, length us, event | category | flops | bytes accessed | tf_op | source)
XLA Modules:
  0.0 109.5 jit_solution(14095504156629051228)
XLA Ops:
  0.6 105.9 %layer.1 = (bf16[128,1024]{1,0:T(8,128)(2,1)}, bf16[128,1024]{1,0:T(8,128)(2,1)}, bf16[128,1024]{1,0:T(8,128)(2,1)}, bf16[128,1024]{1,0:T(8,128)(2,1)}, f32[128,2048]{1,0:T(8,128)}, /*index=5*/f32[2048,128]{1,0:T(8,128)}) custom-call(bf16[128,1024]{1,0:T(8,128)(2,1)} %bitcast.22, bf16[128,1024]{1,0:T(8,128)(2,1)} %bitcast.23, bf16[128,1024]{1,0:T(8,128)(2,1)} %bitcast.24, ...), custom_call_target="tpu_custom_call" | custom-call | flops 9663676416 | bytes 33554432 | tf_op jit(solution)/shard_map/layer/pallas_call | solution.py:499
  106.6 3.0 %outputs.1 = (bf16[128,1024]{1,0:T(8,128)(2,1)}, bf16[128,1024]{1,0:T(8,128)(2,1)}, bf16[128,1024]{1,0:T(8,128)(2,1)}, bf16[128,1024]{1,0:T(8,128)(2,1)}, f32[128,2048]{1,0:T(8,128)}, /*index=5*/f32[2048,128]{1,0:T(8,128)}) custom-call(bf16[128,1024]{1,0:T(8,128)(2,1)} %get-tuple-element.18.refs_0_, bf16[128,1024]{1,0:T(8,128)(2,1)} %get-tuple-element.19.refs_1_, ...), custom_call_target="tpu_custom_call" | custom-call | tf_op jit(solution)/shard_map/outputs/pallas_call | solution.py:551

commit v5 on v4

--- a/solution.py
+++ b/solution.py
@@ -106,14 +106,6 @@
     return copy
 
 
-def join_rows(src, dst, send, recv, me, size):
-    rows = dst.shape[0]
-    width = src.shape[1]
-    copies = [join_block(src, dst, send, recv, me, size, step) for step in range(1, size)]
-    dst[:, rows_of(me, width)] = src[rows_of(me, rows), :]
-    return copies
-
-
 def swap_slots(src, dst, send, recv, me, size):
     cap = src.shape[0] // size
     copies = []
@@ -157,7 +149,7 @@
     q_hbm, k_hbm, v_hbm, routes_ref, gates_ref, up_hbm, down_hbm, cot_ref,
     layer_out, gq_out, gk_out, gv_out, gup_out, gdown_out,
     layer, gq, gk, gv, gup, gdown,
-    qh, kh, vh, heads, att, probs, datt, dheads, gqh, gkh, gvh,
+    qh, kh, vh, heads, att, probs, probs_t, datt, dheads, gqh, gkh, gvh,
     place, sent_grad, grad_in, sent_rows, rows_in, out_rows, dnorm_rows, ret_out, ret_dnorm,
     up, down, dact, act, dpre, rows_t, grad_t,
     gw_own, gw_other, gw_recv, a1_recv, b1_recv, a2_sent, a2_recv, b2_sent, b2_recv,
@@ -242,6 +234,8 @@
     sent_rows[...] = dot_nn(placer, (att_f * inverse).astype(BF16)).astype(BF16)
     row_copies = swap_slots(sent_rows, rows_in, exp_send.at[1], exp_recv.at[1], me_exp, n_exp)
     sent += row_copies
+    for head in range(n_heads):
+        probs_t[head] = probs[head].astype(BF16).T
     arrive(grad_copies)
     load_down.wait()
     load_up.wait()
@@ -361,6 +355,25 @@
     add_core(2)
     core_fourth.wait_recv()
     add_core(3)
+
+    def join_head(src, dst, head, number):
+        cols = slice(head * DH, (head + 1) * DH)
+        there = pl.ds(pl.multiple_of(me_seq * width + head * DH, DH), DH)
+        copies = []
+        for step in range(1, n_seq):
+            peer = lax.rem(me_seq + step, n_seq)
+            copy = remote(
+                src.at[rows_of(peer, rows), cols],
+                dst.at[:, there],
+                seq_send.at[number, step],
+                seq_recv.at[number, step],
+                "seq",
+                peer,
+            )
+            copy.start()
+            copies.append(copy)
+        dst[:, there] = src[rows_of(me_seq, rows), cols]
+        return copies
 
     arrive(dnorm_copies)
     out_copies = swap_slots(out_rows, ret_out, exp_send.at[3], exp_recv.at[3], me_exp, n_exp)
@@ -381,31 +394,35 @@
     arrive(datt_copies)
 
     scaling = 1.0 / math.sqrt(DH)
+    last = []
     for head in range(n_heads):
         cols = slice(head * DH, (head + 1) * DH)
         prob = probs[head]
         dhead = dheads[:, cols]
-        gvh[:, cols] = dot_tn(prob.astype(BF16), dhead).astype(BF16)
         dprobs = dot_nt(dhead, vh[:, cols])
+        gvh[:, cols] = dot_nn(probs_t[head], dhead).astype(BF16)
+        last.append(join_head(gvh, gv, head, 5 + 3 * head))
         delta = jnp.sum(prob * dprobs, axis=-1, keepdims=True)
         dscores = (prob * (dprobs - delta) * scaling).astype(BF16)
+        gqh[:, cols] = dot_nn(dscores, kh[:, cols]).astype(BF16)
+        last.append(join_head(gqh, gq, head, 6 + 3 * head))
         gkh[:, cols] = dot_tn(dscores, qh[:, cols]).astype(BF16)
-        gqh[:, cols] = dot_nn(dscores, kh[:, cols]).astype(BF16)
-    last = []
-    for number, (src, dst) in enumerate(((gvh, gv), (gkh, gk), (gqh, gq)), 5):
-        last += join_rows(src, dst, seq_send.at[number], seq_recv.at[number], me_seq, n_seq)
-    sent += last
-
-    a1[0].wait_recv()
-    a2_sent[...] = (
-        gw_own[2, rows_of(1 - high, piece), :].astype(F32) + a1_recv[1 - high].astype(F32)
-    ).astype(BF16)
-    a2 = reduce_send(a2_sent, a2_recv, 4, peer_high)
-    b1[0].wait_recv()
-    b2_sent[...] = (
-        gw_own[3, rows_of(1 - low, piece), :].astype(F32) + b1_recv[1 - low].astype(F32)
-    ).astype(BF16)
-    b2 = reduce_send(b2_sent, b2_recv, 5, peer_low)
+        last.append(join_head(gkh, gk, head, 7 + 3 * head))
+        if head == 0:
+            a1[0].wait_recv()
+            a2_sent[...] = (
+                gw_own[2, rows_of(1 - high, piece), :].astype(F32)
+                + a1_recv[1 - high].astype(F32)
+            ).astype(BF16)
+            a2 = reduce_send(a2_sent, a2_recv, 4, peer_high)
+            b1[0].wait_recv()
+            b2_sent[...] = (
+                gw_own[3, rows_of(1 - low, piece), :].astype(F32)
+                + b1_recv[1 - low].astype(F32)
+            ).astype(BF16)
+            b2 = reduce_send(b2_sent, b2_recv, 5, peer_low)
+    for copies in last:
+        sent += copies
 
     arrive(out_copies)
     mix = None
@@ -423,8 +440,9 @@
     store(layer, layer_out)
     a1[1].wait_recv()
     b1[1].wait_recv()
-    for number, (src, dst) in enumerate(((gv, gv_out), (gk, gk_out), (gq, gq_out))):
-        arrive(last[number * (n_seq - 1) : (number + 1) * (n_seq - 1)])
+    for number, (src, dst) in enumerate(((gv, gv_out), (gq, gq_out), (gk, gk_out))):
+        for copies in last[number::3]:
+            arrive(copies)
         store(src, dst)
     a2.wait_recv()
     gup[...] = (
@@ -509,6 +527,7 @@
             head_block, head_block, head_block, head_block,
             buf(rows, model),
             buf(width // DH, tokens, tokens, dtype=F32),
+            buf(width // DH, tokens, tokens),
             buf(rows, model),
             head_block, head_block, head_block, head_block,
             buf(TOP, slots, rows),
@@ -527,8 +546,8 @@
             buf(2, piece, hidden),
             buf(2, piece, hidden),
             buf(piece, hidden), buf(piece, hidden), buf(piece, hidden), buf(piece, hidden),
-            dma((8, n_seq)),
-            dma((8, n_seq)),
+            dma((5 + 3 * (width // DH), n_seq)),
+            dma((5 + 3 * (width // DH), n_seq)),
             dma((4, n_exp)),
             dma((4, n_exp)),
             dma((4,)),

time: 110 us -> 109 us (level)
  no operation moved by 1% of the time
where the time goes in v5:
time: 109 us
  Pallas kernels  108 us (99%)
    pallas_call x1, Pallas kernels, shards(): pl.pallas_call(functools.partial(layer_kernel, experts, cap, 512), name='...  105 us
    pallas_call x1, Pallas kernels, shards(): pl.pallas_call(copy_kernel, name='outputs', out_shape=out_shapes, in_spec...  2.97 us

profile of v5, /device:TPU:24, one launch (start us, length us, event | category | flops | bytes accessed | tf_op | source)
XLA Modules:
  0.0 108.6 jit_solution(16757687013603186961)
XLA Ops:
  0.6 105.0 %layer.1 = (bf16[128,1024]{1,0:T(8,128)(2,1)}, bf16[128,1024]{1,0:T(8,128)(2,1)}, bf16[128,1024]{1,0:T(8,128)(2,1)}, bf16[128,1024]{1,0:T(8,128)(2,1)}, f32[128,2048]{1,0:T(8,128)}, /*index=5*/f32[2048,128]{1,0:T(8,128)}) custom-call(bf16[128,1024]{1,0:T(8,128)(2,1)} %bitcast.22, bf16[128,1024]{1,0:T(8,128)(2,1)} %bitcast.23, bf16[128,1024]{1,0:T(8,128)(2,1)} %bitcast.24, ...), custom_call_target="tpu_custom_call" | custom-call | flops 9663676416 | bytes 33554432 | tf_op jit(solution)/shard_map/layer/pallas_call | solution.py:517
  105.6 3.0 %outputs.1 = (bf16[128,1024]{1,0:T(8,128)(2,1)}, bf16[128,1024]{1,0:T(8,128)(2,1)}, bf16[128,1024]{1,0:T(8,128)(2,1)}, bf16[128,1024]{1,0:T(8,128)(2,1)}, f32[128,2048]{1,0:T(8,128)}, /*index=5*/f32[2048,128]{1,0:T(8,128)}) custom-call(bf16[128,1024]{1,0:T(8,128)(2,1)} %get-tuple-element.18.refs_0_, bf16[128,1024]{1,0:T(8,128)(2,1)} %get-tuple-element.19.refs_1_, ...), custom_call_target="tpu_custom_call" | custom-call | tf_op jit(solution)/shard_map/outputs/pallas_call | solution.py:570

commit v6 on v5

--- a/solution.py
+++ b/solution.py
@@ -20,12 +20,10 @@
 
 def gelu_pair(inputs):
     square = inputs * inputs
-    hyper = jnp.tanh(GELU_COEF * inputs * (1.0 + 0.044715 * square))
-    half = 0.5 * (1.0 + hyper)
+    hyper = jnp.tanh(inputs * (GELU_COEF + GELU_COEF * 0.044715 * square))
+    half = 0.5 + 0.5 * hyper
     result = inputs * half
-    slope = half + 0.5 * inputs * (1.0 - hyper * hyper) * GELU_COEF * (
-        1.0 + 3.0 * 0.044715 * square
-    )
+    slope = half + result * (1.0 - hyper) * (GELU_COEF + GELU_COEF * 3.0 * 0.044715 * square)
     return result, slope
 
 
@@ -151,7 +149,7 @@
     layer, gq, gk, gv, gup, gdown,
     qh, kh, vh, heads, att, probs, probs_t, datt, dheads, gqh, gkh, gvh,
     place, sent_grad, grad_in, sent_rows, rows_in, out_rows, dnorm_rows, ret_out, ret_dnorm,
-    up, down, dact, act, dpre, rows_t, grad_t,
+    up, down, up_t, dact, act, dpre, rows_t, grad_t,
     gw_own, gw_other, gw_recv, a1_recv, b1_recv, a2_sent, a2_recv, b2_sent, b2_recv,
     seq_send, seq_recv, exp_send, exp_recv, dp_send, dp_recv, red_send, red_recv, local_sem,
 ):
@@ -246,16 +244,20 @@
         dact[:, cols] = dot_nt(grad_in[...], down[cols, :])
 
     grad_t[...] = grad_in[...].T
+
+    @pl.loop(0, model // 256)
+    def _(c):
+        cols = rows_of(c, 256)
+        up_t[:, cols] = up[cols, :].T
+
     arrive(row_copies)
 
-    @pl.loop(0, hidden // chunk)
-    def _(c):
-        cols = rows_of(c, chunk)
+    for c in range(hidden // chunk):
+        cols = slice(c * chunk, (c + 1) * chunk)
         value, slope = gelu_pair(dot_nn(rows_in[...], up[:, cols]))
         act[:, cols] = value.astype(BF16)
         dpre[:, cols] = (dact[:, cols] * slope).astype(BF16)
 
-    rows_t[...] = rows_in[...].T
     half = model // 2
     piece = half // n_seq
     pair = 2 * piece
@@ -305,30 +307,24 @@
         sent.append(copy)
         return copy
 
+    grads_second(gw_other.at[1], 1 - me_dp, 1 - high)
+    core_second = core_send(1)
+    rows_t[...] = rows_in[...].T
     grads_first(gw_other.at[0], 1 - me_dp, 1 - low)
     core_first = core_send(0)
-    grads_second(gw_other.at[1], 1 - me_dp, 1 - high)
-    core_second = core_send(1)
+    grads_second(gw_own.at[1], me_dp, 1 - high)
     grads_first(gw_own.at[0], me_dp, 1 - low)
-    grads_second(gw_own.at[1], me_dp, 1 - high)
 
     @pl.loop(0, model // 256)
     def _(c):
         cols = rows_of(c, 256)
-        dnorm_rows[:, cols] = dot_nt(dpre[...], up[cols, :]).astype(BF16)
+        dnorm_rows[:, cols] = dot_nn(dpre[...], up_t[:, cols]).astype(BF16)
 
     dnorm_copies = swap_slots(
         dnorm_rows, ret_dnorm, exp_send.at[2], exp_recv.at[2], me_exp, n_exp
     )
     sent += dnorm_copies
 
-    core_first.wait_recv()
-    add_core(0)
-    a1 = []
-    for number, which in enumerate((1 - high, high)):
-        a1.append(
-            reduce_send(gw_own.at[0, rows_of(which, piece), :], a1_recv.at[which], number, peer_low)
-        )
     core_second.wait_recv()
     add_core(1)
     b1 = []
@@ -337,6 +333,13 @@
             reduce_send(
                 gw_own.at[1, rows_of(which, piece), :], b1_recv.at[which], number, peer_high
             )
+        )
+    core_first.wait_recv()
+    add_core(0)
+    a1 = []
+    for number, which in enumerate((1 - high, high)):
+        a1.append(
+            reduce_send(gw_own.at[0, rows_of(which, piece), :], a1_recv.at[which], number, peer_low)
         )
 
     grads_first(gw_other.at[2], 1 - me_dp, low)
@@ -534,6 +537,7 @@
             slot_block, slot_block, slot_block, slot_block,
             slot_block, slot_block, slot_block, slot_block,
             buf(model, hidden),
+            buf(hidden, model),
             buf(hidden, model),
             buf(slots, hidden, dtype=F32),
             buf(slots, hidden),

time: 109 us -> 108 us (level)
  no operation moved by 1% of the time
where the time goes in v6:
time: 108 us
  Pallas kernels  107 us (99%)
    pallas_call x1, Pallas kernels, shards(): pl.pallas_call(functools.partial(layer_kernel, experts, cap, 512), name='...  104 us
    pallas_call x1, Pallas kernels, shards(): pl.pallas_call(copy_kernel, name='outputs', out_shape=out_shapes, in_spec...  2.97 us

profile of v6, /device:TPU:24, one launch (start us, length us, event | category | flops | bytes accessed | tf_op | source)
XLA Modules:
  0.0 107.9 jit_solution(13466970180856994407)
XLA Ops:
  0.6 104.1 %layer.1 = (bf16[128,1024]{1,0:T(8,128)(2,1)}, bf16[128,1024]{1,0:T(8,128)(2,1)}, bf16[128,1024]{1,0:T(8,128)(2,1)}, bf16[128,1024]{1,0:T(8,128)(2,1)}, f32[128,2048]{1,0:T(8,128)}, /*index=5*/f32[2048,128]{1,0:T(8,128)}) custom-call(bf16[128,1024]{1,0:T(8,128)(2,1)} %bitcast.22, bf16[128,1024]{1,0:T(8,128)(2,1)} %bitcast.23, bf16[128,1024]{1,0:T(8,128)(2,1)} %bitcast.24, ...), custom_call_target="tpu_custom_call" | custom-call | flops 9663676416 | bytes 33554432 | tf_op jit(solution)/shard_map/layer/pallas_call | solution.py:520
  104.7 3.0 %outputs.1 = (bf16[128,1024]{1,0:T(8,128)(2,1)}, bf16[128,1024]{1,0:T(8,128)(2,1)}, bf16[128,1024]{1,0:T(8,128)(2,1)}, bf16[128,1024]{1,0:T(8,128)(2,1)}, f32[128,2048]{1,0:T(8,128)}, /*index=5*/f32[2048,128]{1,0:T(8,128)}) custom-call(bf16[128,1024]{1,0:T(8,128)(2,1)} %get-tuple-element.18.refs_0_, bf16[128,1024]{1,0:T(8,128)(2,1)} %get-tuple-element.19.refs_1_, ...), custom_call_target="tpu_custom_call" | custom-call | tf_op jit(solution)/shard_map/outputs/pallas_call | solution.py:574
